TPU v7x, 128 devices: a whole 4x4x4 slice. The times are simulated.
128 devices in a mesh: row: 16 (over z, y), col: 8 (over x, core).
Axes of the slice: x: 4, y: 4, z: 4, core: 2. Of those that a mesh axis runs over, the one named last changes fastest.
Arguments:
- matrix: float32 [2, 8192, 4, 4096], P(None, 'row', None, 'col'), may hold values from -10 to 14, as said below
- inverse_factors: float32 [2, 512, 512], replicated, may hold values from -0.05574408 to 0.05574408
Outputs:
- panels: float32 [2, 2, 8192, 512], P(None, None, 'row')
- updated: float32 [2, 8192, 4, 4096], P(None, 'row', None, 'col')
Inputs may be any that keep to these rules, and one draw needn't show every extreme that they name: Read as an 16384 x 16384 matrix, matrix is symmetric.
All inputs are finite; a program needn't handle non-finite values.
Results may differ from a plain program's by a relative error of at most 0.00012.
Values sent between devices are 32-bit elements; how exact they have to be, the bound alone decides.
No kernel may reach another device: no remote copies, remote signals or barrier semaphores. Data moves between devices by JAX's collectives and lax.ppermute only.
A program may use at most 128 MiB of HBM per device.

v0:
```python
import jax
import jax.numpy as jnp
from jax import lax
from jax.sharding import PartitionSpec as P


def from_root(x, axis, root):
    mine = lax.axis_index(axis) == root
    return lax.psum(jnp.where(mine, x, jnp.zeros_like(x)), axis)


def panel_rows(column, factor, row_blocks, step):
    product = jnp.einsum("anj,ij->ani", column, factor, precision=lax.Precision.HIGHEST)
    return jnp.where((row_blocks >= step)[:, None, None], product, 0.0)


def row_panel_of(current, factor, row_blocks, step, n_col):
    local = step // n_col
    result = from_root(
        panel_rows(current[:, :, local, :], factor, row_blocks, step), "col", step % n_col
    )
    return result


def column_panel(row_panel, ratio, n_col, pcol):
    pieces = [from_root(row_panel, "row", pcol + part * n_col) for part in range(ratio)]
    stacked = jnp.stack(pieces, axis=1)
    return stacked.reshape((-1,) + row_panel.shape[1:])


def trailing(row_panel, col_panel, row_blocks, col_blocks, step):
    update = jnp.einsum("ani,cmi->ancm", row_panel, col_panel, precision=lax.Precision.HIGHEST)
    mask = (row_blocks > step)[:, None, None, None] & (col_blocks > step)[None, None, :, None]
    return jnp.where(mask, update, 0.0)


def body(matrix, inverse_factors):
    rbd = matrix.shape[0]
    cbd = matrix.shape[2]
    n_row = lax.axis_size("row")
    n_col = lax.axis_size("col")
    ratio = n_row // n_col
    prow = lax.axis_index("row")
    pcol = lax.axis_index("col")
    row_blocks = jnp.arange(rbd, dtype=jnp.int32) * n_row + prow
    col_blocks = jnp.arange(cbd, dtype=jnp.int32) * n_col + pcol
    current = matrix
    panels = []
    for step in range(2):
        rows_now = row_panel_of(current, inverse_factors[step], row_blocks, step, n_col)
        cols_now = column_panel(rows_now, ratio, n_col, pcol)
        current = current - trailing(rows_now, cols_now, row_blocks, col_blocks, step)
        panels.append(rows_now)
    return (jnp.stack(panels), current)


def solution(mesh):
    placed = (P(None, "row", None, "col"), P())
    return jax.shard_map(
        body,
        mesh=mesh,
        in_specs=placed,
        out_specs=(P(None, None, "row", None), P(None, "row", None, "col")),
        check_vma=False,
    )
```

profile of v0, /device:TPU:21, one launch (start us, length us, event | category | flops | bytes accessed | tf_op | source)
XLA Modules:
  0.0 439.8 jit_solution(8666622533113412183)
XLA Ops:
  7.2 1.6 slice-done.2
  8.8 6.0 %select_select_fusion.1 = f32[2,512,512]{2,1,0:T(8,128)} fusion(f32[2,512,1,512]{3,2,1,0:T(1,128)S(1)} %slice-done.2, f32[2,512,512]{2,1,0:T(8,128)} %param.3, pred[2]{0:T(512)(128)(4,1)S(1)} %broadcast_compare_fusion.3, pred[]{:T(512)S(6)} %eq.14), kind=kOutput, calls=%fused_computation.16 | convolution fusion | flops 3222274048 | bytes 5242883 | tf_op jit(solution)/shard_map/anj,ij->ani/dot_general | solution.py:13
  14.9 64.6 %all-reduce.7.cloned.1.call-done = f32[2,512,512]{2,1,0:T(8,128)} async-done(((f32[2,512,512]{2,1,0:T(8,128)}), f32[2,512,512]{2,1,0:T(8,128)}) %all-reduce.7.cloned.1.call-update) | async-done | bytes 2097168 | tf_op jit(solution)/shard_map/psum | solution.py:9
  79.5 4.3 select_bitcast_fusion.3
  83.9 0.2 all-reduce.9.cloned.1.call-start
  84.1 0.1 broadcast_and_fusion.1
  84.2 106.4 %all-reduce.13.cloned.1.call-done = (f32[2,1,512,512]{3,2,0,1:T(8,128)}, f32[2,1,512,512]{3,2,0,1:T(8,128)}) async-done(((f32[2,1,512,512]{3,2,0,1:T(8,128)}, f32[2,1,512,512]{3,2,0,1:T(8,128)}), (f32[2,1,512,512]{3,2,0,1:T(8,128)}, f32[2,1,512,512]{3,2,0,1:T(8,128)})) %all-reduce.13.cloned.1.call-update) | async-done | bytes 4194320 | tf_op jit(solution)/shard_map/psum | solution.py:9
  190.6 2.7 pad_maximum_fusion
  193.3 0.4 copy.8
  193.7 1.1 copy-done.1
  194.9 22.8 %copy_subtract_fusion = f32[2,512,4,512]{3,1,2,0:T(8,128)S(1)} fusion(f32[2,512,4,512]{3,2,1,0:T(4,128)} %param.2, pred[2,4]{1,0:T(4,128)(4,1)S(1)} %broadcast_and_fusion.1, f32[4,512,512,1]{2,1,0,3:T(8,128)S(1)} %bitcast.51, f32[2,512,512]{2,1,0:T(8,128)S(1)} %copy-done.1), kind=kOutput, calls=%fused_computation | convolution fusion | flops 12889096192 | bytes 23068680 | tf_op jit(solution)/shard_map/ani,cmi->ancm/dot_general | solution.py:32
  217.7 3.4 copy-done
  221.0 4.8 %select_select_fusion = f32[2,512,512]{2,1,0:T(8,128)} fusion(f32[2,512,4,512]{3,1,2,0:T(8,128)S(1)} %copy_subtract_fusion, f32[2,512,512]{2,1,0:T(8,128)S(1)} %copy-done.3, pred[2]{0:T(512)(128)(4,1)S(1)} %get-tuple-element.14, pred[]{:T(512)S(6)} %eq.15), kind=kOutput, calls=%fused_computation.13 | convolution fusion | flops 3222274048 | bytes 5243393 | tf_op jit(solution)/shard_map/anj,ij->ani/dot_general | solution.py:13
  225.9 62.1 %all-reduce.9.cloned.1.call-done = f32[2,512,512]{2,1,0:T(8,128)} async-done(((f32[2,512,512]{2,1,0:T(8,128)}), f32[2,512,512]{2,1,0:T(8,128)}) %all-reduce.9.cloned.1.call-update) | async-done | bytes 2097168 | tf_op jit(solution)/shard_map/psum | solution.py:9
  288.1 4.3 select_bitcast_fusion.1
  292.5 4.2 pad_maximum_fusion.1
  296.8 102.4 %all-reduce.11.cloned.1.call-done = (f32[2,1,512,512]{3,2,0,1:T(8,128)}, f32[2,1,512,512]{3,2,0,1:T(8,128)}) async-done(((f32[2,1,512,512]{3,2,0,1:T(8,128)}, f32[2,1,512,512]{3,2,0,1:T(8,128)}), (f32[2,1,512,512]{3,2,0,1:T(8,128)}, f32[2,1,512,512]{3,2,0,1:T(8,128)})) %all-reduce.11.cloned.1.call-update) | async-done | bytes 4194320 | tf_op jit(solution)/shard_map/psum | solution.py:9
  399.2 2.8 pad_maximum_fusion.2
  402.0 0.4 copy.10
  402.5 0.1 slice-done
  402.6 1.7 slice-done.1
  404.4 0.6 copy-done.2
  404.9 16.2 %select_subtract_fusion = f32[2,512,4,512]{3,1,2,0:T(8,128)} fusion(f32[2,512,4,512]{3,1,2,0:T(8,128)S(1)} %bitcast.47, pred[2,4]{1,0:T(4,128)(4,1)S(1)} %broadcast_and_fusion, f32[4,512,512,1]{2,1,0,3:T(8,128)S(1)} %bitcast.48, f32[2,512,512]{2,1,0:T(8,128)S(1)} %copy-done.2), kind=kOutput, calls=%fused_computation.1 | convolution fusion | flops 12889096192 | bytes 23068680 | tf_op jit(solution)/shard_map/ani,cmi->ancm/dot_general | solution.py:32
  421.1 12.2 %copy.11 = f32[2,512,4,512]{3,2,1,0:T(4,128)} copy(f32[2,512,4,512]{3,1,2,0:T(8,128)} %select_subtract_fusion) | data formatting | bytes 16777216
  (22 shorter events, 0.3 us)
Async XLA Ops:
  7.2 72.4 %all-reduce.7.cloned.1.call-start = ((), (), s32[]{:S(2)}) async-start(), calls=%async_computation | async-start | bytes 4194304 | tf_op jit(solution)/shard_map/psum | solution.py:9
  7.2 1.6 slice-start.2
  14.9 175.7 %all-reduce.13.cloned.1.call-start = ((), (), s32[]{:S(2)}) async-start(), calls=%async_computation.3 | async-start | bytes 8388608 | tf_op jit(solution)/shard_map/psum | solution.py:9
  83.9 204.2 %all-reduce.9.cloned.1.call-start = ((), (), s32[]{:S(2)}) async-start(), calls=%async_computation.1 | async-start | bytes 4194304 | tf_op jit(solution)/shard_map/psum | solution.py:9
  193.3 1.6 copy-start.1
  194.9 26.2 %copy-start.3 = (f32[2,512,512]{2,1,0:T(8,128)S(1)}, f32[2,512,512]{2,1,0:T(8,128)}, u32[]{:S(2)}) copy-start(f32[2,512,512]{2,1,0:T(8,128)} %param.3) | copy-start | bytes 6291460
  217.6 3.4 copy-start
  225.9 173.3 %all-reduce.11.cloned.1.call-start = ((), (), s32[]{:S(2)}) async-start(), calls=%async_computation.2 | async-start | bytes 8388608 | tf_op jit(solution)/shard_map/psum | solution.py:9
  399.2 3.4 slice-start
  402.0 2.3 slice-start.1
  402.0 2.9 copy-start.2
Sparse Core Ops, SparseCore 0:
  15.0 64.5 all-reduce.6
  84.0 106.5 all-reduce.12
  226.0 62.0 all-reduce.8
  292.5 106.5 all-reduce.10
where the time goes:
time: 441 us; the launch traced here: 440 us
  waiting for transfers between devices  336 us (76%)
  matrix products  49.7 us (11%)
  local copies, waits for them, and re-layouts  21.6 us (5%)
  other arithmetic  18.6 us (4%)
  between operations  13.9 us (3%)
    psum x4, waiting for transfers between devices, from_root(): return lax.psum(jnp.where(mine, x, jnp.zeros_like(x)), axis)  336 us
    dot_general x2, matrix products, trailing(): jnp.einsum('ani,cmi->ancm', row_panel, col_panel, precision=lax.Precision...  38.9 us
    unnamed x13, local copies, waits for them, and re-layouts  19.2 us
    another operation x4, other arithmetic, column_panel(): stacked = jnp.stack(pieces, axis=1)  14.1 us
    dot_general x2, matrix products, panel_rows(): jnp.einsum('anj,ij->ani', column, factor, precision=lax.Precision.HIGHEST)  10.8 us
  transfers between devices with their start and end apart: 4, of which 4 were waited for; matrix products, arithmetic and copies ran while one was open for 1% of the time, Pallas kernels for 0%

commit v1 on v0

v1 whole, which is shorter than its diff:
```python
import functools

import jax
import jax.numpy as jnp
from jax import lax
from jax.experimental import pallas as pl
from jax.experimental.pallas import tpu as pltpu
from jax.sharding import PartitionSpec as P

AXES = ("row", "col")
RING = 4
MOVES = (1, -1, 2)
VMEM_BYTES = 50 * 1024 * 1024
NN = (((1,), (0,)), ((), ()))
NT = (((1,), (1,)), ((), ()))


def place(z, y, x, c):
    return ((z % RING) * RING + y % RING) * (2 * RING) + (x % RING) * 2 + c


def pairs(target):
    found = []
    for z in range(RING):
        for y in range(RING):
            for x in range(RING):
                for c in range(2):
                    to = target(z, y, x, c)
                    if to is not None:
                        found.append((place(z, y, x, c), place(*to)))
    return found


def everyone(z, y, x, c):
    return True


def along_u(d, wanted=everyone):
    def target(z, y, x, c):
        if not wanted(z, y, x, c):
            return None
        return (z, y + d, x, c) if c == 0 else (z + d, y, x, c)

    return pairs(target)


def along_v(d, wanted=everyone):
    def target(z, y, x, c):
        if not wanted(z, y, x, c):
            return None
        return (z + d, y, x, c) if c == 0 else (z, y + d, x, c)

    return pairs(target)


def send(x, moves):
    return lax.ppermute(x, AXES, moves)


def other_core(x):
    return send(x, pairs(lambda z, y, x, c: (z, y, x, 1 - c)))


def choose(index, *options):
    result = options[-1]
    for i in range(len(options) - 2, -1, -1):
        result = jnp.where(index == i, options[i], result)
    return result


def ring_order(index, own, got):
    shape = (own.shape[0], RING) + own.shape[1:]
    whole = jnp.zeros(shape, own.dtype)
    for d, value in ((0, own), (-1, got[1]), (1, got[-1]), (2, got[2])):
        start = (0, (index + d) % RING) + (0,) * (len(shape) - 2)
        whole = lax.dynamic_update_slice(whole, value[:, None], start)
    return whole.reshape((own.shape[0], RING * own.shape[1]) + own.shape[2:])


def split(x):
    high = x.astype(jnp.bfloat16)
    low = (x - high.astype(jnp.float32)).astype(jnp.bfloat16)
    return high, low


def dot3(a, b, dims):
    a_high, a_low = a
    b_high, b_low = b
    one = functools.partial(
        lax.dot_general, dimension_numbers=dims, preferred_element_type=jnp.float32
    )
    return one(a_high, b_high) + (one(a_high, b_low) + one(a_low, b_high))


def factors_kernel(
    where_ref, mine_ref, theirs_ref, corner_ref, inv_ref,
    panels_ref, yg_high, yg_low, ye_high, ye_low,
    inv_high, inv_low, p01_high, p01_low, f_high, f_low,
):
    a = pl.program_id(0)
    prow, pcol, core = where_ref[0], where_ref[1], where_ref[2]
    part = yg_high.shape[2] // 2

    @pl.when((a == 0) & (pl.program_id(1) == 0))
    def _():
        for i in range(2):
            inv_high[i], inv_low[i] = split(inv_ref[i])
        inv0 = inv_high[0], inv_low[0]
        p01 = split(dot3(split(corner_ref[...]), inv0, NT))
        p01_high[...], p01_low[...] = p01
        f_high[...], f_low[...] = split(dot3(p01, inv0, NN))

    inv0 = inv_high[0], inv_low[0]
    inv1 = inv_high[1], inv_low[1]
    mine, theirs = mine_ref[0], theirs_ref[0]
    left = jnp.where(core == 0, mine, theirs)
    right = jnp.where(core == 0, theirs, mine)
    block = a * 16 + prow
    p0 = dot3(split(left), inv0, NT)
    p0_parts = split(p0)
    below = right - dot3(p0_parts, (p01_high[...], p01_low[...]), NT)
    p1 = jnp.where(block >= 1, dot3(split(below), inv1, NT), 0.0)
    panels_ref[0, 0] = p0
    panels_ref[1, 0] = p1
    z0 = jnp.where(block >= 1, dot3(p0_parts, inv0, NN), 0.0)
    y1 = jnp.where(block >= 2, dot3(split(p1), inv1, NN), 0.0)
    y0 = z0 - dot3(split(y1), (f_high[...], f_low[...]), NN)
    e0 = jnp.where(pcol == 0, 0.0, jnp.where(pcol == 1, z0, y0))
    e1 = jnp.where(pcol <= 1, 0.0, y1)
    for high, low, first, second in ((yg_high, yg_low, y0, y1), (ye_high, ye_low, e0, e1)):
        for k in range(RING):
            for i, value in enumerate((first, second)):
                h, l = split(value[:, k * part : (k + 1) * part])
                high[k, :, i * part : (i + 1) * part] = h
                low[k, :, i * part : (i + 1) * part] = l


def row_factors(where, mine, theirs, corner, inverse_factors):
    rbd, nb, _ = mine.shape
    tile = nb // 2
    rows = pl.BlockSpec((1, tile, nb), lambda a, t: (a, t, 0))
    parts = pl.BlockSpec((RING, tile, nb // 2), lambda a, t: (0, a * 2 + t, 0))
    parts_shape = jax.ShapeDtypeStruct((RING, rbd * nb, nb // 2), jnp.bfloat16)
    half = pltpu.VMEM((nb, nb), jnp.bfloat16)
    return pl.pallas_call(
        factors_kernel,
        grid=(rbd, 2),
        in_specs=[
            pl.BlockSpec(memory_space=pltpu.SMEM),
            rows,
            rows,
            pl.BlockSpec((nb, nb), lambda a, t: (0, 0)),
            pl.BlockSpec((2, nb, nb), lambda a, t: (0, 0, 0)),
        ],
        out_specs=[pl.BlockSpec((2, 1, tile, nb), lambda a, t: (0, a, t, 0))] + [parts] * 4,
        out_shape=[jax.ShapeDtypeStruct((2, rbd, nb, nb), jnp.float32)] + [parts_shape] * 4,
        scratch_shapes=[pltpu.VMEM((2, nb, nb), jnp.bfloat16)] * 2 + [half] * 4,
        compiler_params=pltpu.CompilerParams(vmem_limit_bytes=VMEM_BYTES),
        cost_estimate=pl.CostEstimate(flops=20 * 10**9, bytes_accessed=24 * 2**20, transcendentals=0),
    )(where, mine, theirs, corner, inverse_factors)


def update_kernel(count, ks_ref, x_ref, yg_high, yg_low, ye_high, ye_low, *rest):
    pieces, out_ref, rhs = rest[:count], rest[count], rest[count + 1]
    rows = yg_high.shape[1]
    depth = yg_high.shape[2]
    cbd = rhs.shape[0]
    lanes = rhs.shape[2] // RING
    stride = RING * cbd

    @pl.when((pl.program_id(0) == 0) & (pl.program_id(1) == 0))
    def _():
        for j in range(count):
            for c in range(cbd):
                for t in range(RING):
                    high, low = split(pieces[j][pl.ds(t * cbd + c, depth, stride=stride), :])
                    for place_at, value in ((0, high), (1, low), (2, high)):
                        start = (3 * j + place_at) * depth
                        rhs[c, start : start + depth, t * lanes : (t + 1) * lanes] = value

    left = []
    for high, low in ((ye_high, ye_low), (yg_high, yg_low)):
        terms = []
        for j in range(count):
            h, l = high[ks_ref[j]], low[ks_ref[j]]
            terms += [h, h, l]
        left.append(jnp.concatenate(terms, axis=1))
    for c in range(cbd):
        product = jnp.dot(left[min(c, 1)], rhs[c], preferred_element_type=jnp.float32)
        for t in range(RING):
            at = pl.ds(t * cbd + c, rows, stride=stride)
            out_ref[at, :] = x_ref[at, :] - product[:, t * lanes : (t + 1) * lanes]


def subtract_products(lines, factors, ks, pieces, cbd):
    nb = 2 * factors[0].shape[2]
    rbd = factors[0].shape[1] // nb
    count = len(pieces)
    tile = nb // 2
    block = pl.BlockSpec((tile * RING * cbd, lines.shape[1]), lambda a, t: (a * 2 + t, 0))
    parts = pl.BlockSpec((RING, tile, nb // 2), lambda a, t: (0, a * 2 + t, 0))
    whole = pl.BlockSpec(
        pieces[0].shape, lambda a, t: (0, 0), pipeline_mode=pl.Buffered(buffer_count=1)
    )
    return pl.pallas_call(
        functools.partial(update_kernel, count),
        grid=(rbd, 2),
        in_specs=[pl.BlockSpec(memory_space=pltpu.SMEM), block] + [parts] * 4 + [whole] * count,
        out_specs=block,
        out_shape=jax.ShapeDtypeStruct(lines.shape, lines.dtype),
        scratch_shapes=[pltpu.VMEM((cbd, 3 * count * (nb // 2), nb), jnp.bfloat16)],
        compiler_params=pltpu.CompilerParams(vmem_limit_bytes=VMEM_BYTES),
        cost_estimate=pl.CostEstimate(
            flops=3 * count * 11 * 10**8, bytes_accessed=(16 + 4 + 2 * count) * 2**20, transcendentals=0
        ),
    )(ks, lines, *factors, *pieces)


def column_kernel(x_ref, out_ref):
    rows, nb = out_ref.shape[1:]
    lanes = nb // RING
    cbd = x_ref.shape[0] // rows // RING
    for t in range(RING):
        at = pl.ds(t * cbd, rows, stride=RING * cbd)
        out_ref[0, :, t * lanes : (t + 1) * lanes] = x_ref[at, :]


def first_column(lines, rbd, nb, cbd):
    tile = nb // 2
    return pl.pallas_call(
        column_kernel,
        grid=(rbd, 2),
        in_specs=[pl.BlockSpec((tile * RING * cbd, lines.shape[1]), lambda a, t: (a * 2 + t, 0))],
        out_specs=pl.BlockSpec((1, tile, nb), lambda a, t: (a, t, 0)),
        out_shape=jax.ShapeDtypeStruct((rbd, nb, nb), lines.dtype),
        cost_estimate=pl.CostEstimate(flops=0, bytes_accessed=10 * 2**20, transcendentals=0),
    )(lines)


def corner_kernel(core_ref, x_ref, out_ref):
    half, nb = out_ref.shape
    lanes = nb // RING
    cbd = x_ref.shape[0] // nb // RING
    stride = RING * cbd

    @pl.when(core_ref[0] == 0)
    def _():
        for t in range(RING):
            out_ref[:, t * lanes : (t + 1) * lanes] = x_ref[pl.ds(t * cbd, half, stride=stride), :]

    @pl.when(core_ref[0] != 0)
    def _():
        for t in range(RING // 2):
            at = pl.ds((t + RING // 2) * cbd, nb, stride=stride)
            out_ref[t * lanes : (t + 1) * lanes, :] = x_ref[at, :].T


def corner_half(core, lines, nb, cbd):
    return pl.pallas_call(
        corner_kernel,
        grid=(1,),
        in_specs=[
            pl.BlockSpec(memory_space=pltpu.SMEM),
            pl.BlockSpec((nb * RING * cbd, lines.shape[1]), lambda i: (0, 0)),
        ],
        out_specs=pl.BlockSpec((nb // 2, nb), lambda i: (0, 0)),
        out_shape=jax.ShapeDtypeStruct((nb // 2, nb), lines.dtype),
        compiler_params=pltpu.CompilerParams(vmem_limit_bytes=VMEM_BYTES),
        cost_estimate=pl.CostEstimate(flops=0, bytes_accessed=5 * 2**20, transcendentals=0),
    )(core, lines)


def to_lines(matrix):
    rbd, rows, cbd, nb = matrix.shape
    cut = matrix.reshape(rbd, rows, cbd, RING, nb // RING)
    return cut.transpose(0, 1, 3, 2, 4).reshape(-1, nb // RING)


def from_lines(lines, shape):
    rbd, rows, cbd, nb = shape
    cut = lines.reshape(rbd, rows, RING, cbd, nb // RING)
    return cut.transpose(0, 1, 3, 2, 4).reshape(shape)


def share(x, index, first, second):
    one = send(x, first)
    two = send(jnp.where(index == 0, x, one), second)
    return choose(index, x, one, two, two)


def top_rows(lines, u, v, c):
    part = lines.shape[0] // 2 // RING
    small = part // RING

    def rows(k):
        return lax.dynamic_slice_in_dim(lines, (k % RING) * part, part)

    def root(z, y, x, c):
        return z == 0 and y < 2

    got = {d: send(rows(u + d), along_u(d, root)) for d in MOVES}
    own = rows(u)

    def quarter(d):
        begin = ((v + d) % RING) * small
        o, p, q, m = (
            lax.dynamic_slice_in_dim(t, begin, small) for t in (own, got[1], got[2], got[-1])
        )
        return jnp.stack([choose(u, o, p, q, m), choose(u, m, o, p, q)])

    def holder(z, y, x, c):
        return z == 0 if c == 0 else y < 2

    mine = quarter(0)
    sent = {d: send(quarter(d), along_v(d, holder)) for d in MOVES}
    part_a = choose(v, mine[0], sent[1][0], sent[2][0], sent[-1][0])
    part_b = jnp.where(
        c == 0,
        choose(v, mine[1], sent[1][1], sent[2][1], sent[-1][1]),
        choose(v, sent[-1][0], mine[0], sent[1][0], sent[2][0]),
    )
    piece = jnp.stack([part_a, part_b])
    whole = ring_order(v, piece, {d: send(piece, along_v(d)) for d in MOVES})

    before = send(whole, along_u(1))
    after = send(whole, along_u(-1))
    far_a = send(before[0], along_u(1))
    far_b = send(after[1], along_u(-1))
    far = jnp.concatenate([far_a, far_b])
    lanes = lines.shape[1]
    return [t.reshape(-1, lanes) for t in (whole, before, after, far)]


def row_inputs(column, start, u, v, x, c):
    def sign(c):
        return 1 if c == 0 else -1

    def x_first(z, y, x, c):
        return (z, y, sign(c), c) if x == 0 else None

    def x_second(z, y, x, c):
        if x == 0:
            return (z, y, -sign(c), c)
        return (z, y, 2, c) if x == sign(c) % RING else None

    s = jnp.where(c == 0, x, -x) % RING
    start = share(start, s, pairs(x_first), pairs(x_second))
    mine = share(column, s, pairs(x_first), pairs(x_second))
    theirs = other_core(mine)

    def uv(z, y, c):
        return (y, z) if c == 0 else (z, y)

    def zyxc(u, v, x, c):
        return (v, u, x, c) if c == 0 else (u, v, x, c)

    def v_first(z, y, x, c):
        u, v = uv(z, y, c)
        return zyxc(u, 1, x, c) if v == 0 and u == 1 - c else None

    def v_second(z, y, x, c):
        u, v = uv(z, y, c)
        return zyxc(u, 3 if v == 0 else 2, x, c) if v < 2 and u == 1 - c else None

    def u_first(z, y, x, c):
        u, v = uv(z, y, c)
        return zyxc(u + 1, v, x, c) if u == 1 - c else None

    def u_second(z, y, x, c):
        u, v = uv(z, y, c)
        w = (u - 1 + c) % RING
        return zyxc(u - 1 if w == 0 else u + 1, v, x, c) if w < 2 else None

    line = share(start, v, pairs(v_first), pairs(v_second))
    here = share(line, (u - 1 + c) % RING, pairs(u_first), pairs(u_second))
    there = other_core(here)
    corner = jnp.concatenate([jnp.where(c == 0, here, there), jnp.where(c == 0, there, here)])
    return mine, theirs, corner


def body(matrix, inverse_factors):
    rbd, nb, cbd, _ = matrix.shape
    prow = lax.axis_index("row")
    pcol = lax.axis_index("col")
    z, y = prow // RING, prow % RING
    x, c = pcol // 2, pcol % 2
    u = jnp.where(c == 0, y, z)
    v = jnp.where(c == 0, z, y)

    lines = to_lines(matrix)
    own, before, after, far = top_rows(lines, u, v, c)
    start = corner_half(c.astype(jnp.int32)[None], lines, nb, cbd)
    mine, theirs, corner = row_inputs(first_column(lines, rbd, nb, cbd), start, u, v, x, c)

    where = jnp.stack([prow, pcol, c]).astype(jnp.int32)
    panels, *factors = row_factors(where, mine, theirs, corner, inverse_factors)
    ks = jnp.stack([u, u - 1, u + 1, u + 2]).astype(jnp.int32) % RING
    partial = subtract_products(lines, factors, ks[:3], (own, before, after), cbd)
    final = subtract_products(partial, factors, ks[3:], (far,), cbd)
    return panels, from_lines(final, matrix.shape)


def solution(mesh):
    return jax.shard_map(
        body,
        mesh=mesh,
        in_specs=(P(None, "row", None, "col"), P()),
        out_specs=(P(None, None, "row", None), P(None, "row", None, "col")),
        check_vma=False,
    )
```

time: 441 us -> 199 us (0.45)
  waiting for transfers between devices: 336 us -> 66.2 us
  Pallas kernels: 0 us -> 63.3 us
  matrix products: 49.7 us -> 0 us
  starting transfers between devices: 0.34 us -> 37.4 us
  between operations: 13.9 us -> 1.26 us
  local copies, waits for them, and re-layouts: 21.6 us -> 12.2 us
    psum x4 -> x0, waiting for transfers between devices: 336 us -> none  [from_root(): return lax.psum(jnp.where(mine, x, jnp.zeros_like(x)), axis)]
    ppermute x0 -> x23, waiting for transfers between devices: none -> 66.2 us  [send(): return lax.ppermute(x, AXES, moves)]
    pallas_call x0 -> x5, Pallas kernels: none -> 63.3 us  [the longest x2 36.5 us: subtract_products(): pl.pallas_call(functools.partial(update_kernel, count), grid=(rbd, 2), in...]
    dot_general x4 -> x0, matrix products: 49.7 us -> none  [the longest x2 38.9 us: trailing(): jnp.einsum('ani,cmi->ancm', row_panel, col_panel, precision=lax.Precision...]
    ppermute x0 -> x23, starting transfers between devices: none -> 37.4 us  [send(): return lax.ppermute(x, AXES, moves)]
    unnamed x13 -> x6, local copies, waits for them, and re-layouts: 19.2 us -> 1.35 us
    another operation x5 -> x8, other arithmetic: 18.4 us -> 7.21 us  [the longest x4 4.1 us: quarter(): return jnp.stack([choose(u, o, p, q, m), choose(u, m, o, p, q)])]
    select_n x0 -> x10, other arithmetic: none -> 6.61 us  [the longest x4 3.64 us: share(): two = send(jnp.where(index == 0, x, one), second)]
  transfers between devices with their start and end apart: 4 -> 23, of which waited for: 4 -> 10; matrix products, arithmetic and copies ran while one was open for 1% -> 12% of each run, Pallas kernels for 0% -> 4%
where the time goes in v1:
time: 199 us; the launch traced here: 196 us
  waiting for transfers between devices  66.2 us (33%)
  Pallas kernels  63.3 us (32%)
  starting transfers between devices  37.4 us (19%)
  other arithmetic  16.2 us (8%)
  local copies, waits for them, and re-layouts  12.2 us (6%)
    ppermute x23, waiting for transfers between devices, send(): return lax.ppermute(x, AXES, moves)  66.2 us
    ppermute x23, starting transfers between devices, send(): return lax.ppermute(x, AXES, moves)  37.4 us
    pallas_call x2, Pallas kernels, subtract_products(): pl.pallas_call(functools.partial(update_kernel, count), grid=(rbd, 2), in...  36.5 us
    pallas_call x1, Pallas kernels, row_factors(): pl.pallas_call(factors_kernel, grid=(rbd, 2), in_specs=[pl.BlockSpec(memo...  18.8 us
    pallas_call x1, Pallas kernels, first_column(): pl.pallas_call(column_kernel, grid=(rbd, 2), in_specs=[pl.BlockSpec((tile...  5.54 us
    another operation x4, other arithmetic, quarter(): return jnp.stack([choose(u, o, p, q, m), choose(u, m, o, p, q)])  4.1 us
  transfers between devices with their start and end apart: 23, of which 10 were waited for; matrix products, arithmetic and copies ran while one was open for 12% of the time, Pallas kernels for 4%

profile of v1, /device:TPU:21, one launch (start us, length us, event | category | flops | bytes accessed | tf_op | source)
XLA Modules:
  0.0 196.5 jit_solution(18319338744969575331)
XLA Ops:
  0.7 3.6 %constant_dynamic-slice_fusion.2 = (f32[2048,128]{1,0:T(8,128)}, f32[2048,128]{1,0:T(8,128)}, f32[2048,128]{1,0:T(8,128)}) fusion(f32[16384,128]{1,0:T(8,128)} %bitcast.85, s32[]{:T(128)S(6)} %select_n.428, s32[]{:T(128)S(6)} %select_n.433, s32[]{:T(128)S(6)} %select_n.431), kind=kLoop, calls=%fused_computation.41 | loop fusion | bytes 6291468 | tf_op jit(solution)/shard_map/dynamic_slice | solution.py:296
  5.8 1.7 collective-permute-start.11
  7.5 5.5 %shard_map.41 = f32[2,512,512]{2,1,0:T(8,128)} custom-call(f32[16384,128]{1,0:T(8,128)} %bitcast.86), custom_call_target="tpu_custom_call" | custom-call | bytes 10485760 | tf_op jit(solution)/shard_map/pallas_call | solution.py:230
  13.0 2.0 %collective-permute-start = (f32[2,512,512]{2,1,0:T(8,128)}, f32[2,512,512]{2,1,0:T(8,128)}, u32[]{:S(2)}, u32[]{:S(2)}) collective-permute-start(f32[2,512,512]{2,1,0:T(8,128)} %shard_map.41), channel_id=1, source_target_pairs={{0,2},{1,7},{8,10},{9,15},{16,18},{17,23},{24,26},{25,31},{32,34},... | collective-permute-start | bytes 6291464 | tf_op jit(solution)/shard_map/ppermute | solution.py:57
  15.0 2.5 %shard_map.42 = f32[256,512]{1,0:T(8,128)S(1)} custom-call(s32[1]{0:T(128)} %bitcast.2.core_ref, f32[16384,128]{1,0:T(8,128)} %bitcast.87), custom_call_target="tpu_custom_call" | custom-call | bytes 5242880 | tf_op jit(solution)/shard_map/pallas_call | solution.py:259
  18.4 1.6 select_bitcast_fusion.6
  28.0 16.6 %collective-permute-done.14 = f32[2,512,128]{2,1,0:T(8,128)} collective-permute-done((f32[2,512,128]{2,1,0:T(8,128)}, f32[2,512,128]{2,1,0:T(8,128)}, u32[]{:S(2)}, u32[]{:S(2)}) %collective-permute-start.14) | collective-permute-done | bytes 524320 | tf_op jit(solution)/shard_map/ppermute | solution.py:57
  44.7 5.5 %collective-permute-done.13 = f32[2,512,128]{2,1,0:T(8,128)} collective-permute-done((f32[2,512,128]{2,1,0:T(8,128)}, f32[2,512,128]{2,1,0:T(8,128)}, u32[]{:S(2)}, u32[]{:S(2)}) %collective-permute-start.13) | collective-permute-done | bytes 524320 | tf_op jit(solution)/shard_map/ppermute | solution.py:57
  50.2 1.6 fusion.4
  53.3 2.7 %collective-permute-done.4 = f32[256,512]{1,0:T(8,128)S(1)} collective-permute-done((f32[256,512]{1,0:T(8,128)S(1)}, f32[256,512]{1,0:T(8,128)S(1)}, u32[]{:S(2)}, u32[]{:S(2)}) %collective-permute-start.4) | collective-permute-done | bytes 524320 | tf_op jit(solution)/shard_map/ppermute | solution.py:57
  57.0 6.5 %collective-permute-start.17 = (f32[2,512,128]{2,1,0:T(8,128)S(1)}, f32[2,512,128]{2,1,0:T(8,128)S(1)}, u32[]{:S(2)}, u32[]{:S(2)}) collective-permute-start(f32[2,512,128]{2,1,0:T(8,128)S(1)} %pad_maximum_fusion.5), channel_id=1, source_target_pairs={{0,96},{1,25},{2,98},{3,27},{4,100},{5,29},{6,102},{7,31},{8,104},... | collective-permute-start | bytes 1572872 | tf_op jit(solution)/shard_map/ppermute | solution.py:57
  63.4 1.9 collective-permute-start.18
  65.3 1.5 broadcast_in_dim.16
  67.7 3.4 %broadcast_select_fusion = f32[2,512,512]{2,1,0:T(8,128)} fusion(f32[2,512,512]{2,1,0:T(8,128)S(1)} %copy-done, f32[2,512,512]{2,1,0:T(8,128)} %collective-permute-done, pred[]{:T(512)S(6)} %eq.41), kind=kLoop, calls=%fused_computation.5 | loop fusion | flops 524288 | bytes 6291457 | tf_op jit(solution)/shard_map/jit(_where)/select_n | solution.py:287
  73.2 1.9 collective-permute-done.17
  80.5 10.9 %collective-permute-done.6 = f32[256,512]{1,0:T(8,128)S(1)} collective-permute-done((f32[256,512]{1,0:T(8,128)S(1)}, f32[256,512]{1,0:T(8,128)S(1)}, u32[]{:S(2)}, u32[]{:S(2)}) %collective-permute-start.6) | collective-permute-done | bytes 524320 | tf_op jit(solution)/shard_map/ppermute | solution.py:57
  92.9 16.4 %collective-permute-done.7 = f32[256,512]{1,0:T(8,128)S(1)} collective-permute-done((f32[256,512]{1,0:T(8,128)S(1)}, f32[256,512]{1,0:T(8,128)S(1)}, u32[]{:S(2)}, u32[]{:S(2)}) %collective-permute-start.7) | collective-permute-done | bytes 524320 | tf_op jit(solution)/shard_map/ppermute | solution.py:57
  110.7 2.4 %select_select_fusion.mine_ref = f32[2,512,512]{2,1,0:T(8,128)S(1)} fusion(f32[2,512,512]{2,1,0:T(8,128)S(1)} %copy-done, f32[2,512,512]{2,1,0:T(8,128)} %collective-permute-done, f32[2,512,512]{2,1,0:T(8,128)} %collective-permute-done.1, pred[]{:T(512)S(6)} %eq.42, pred[]{:T(512)S(6)} %eq.41), kind=kLoop, calls=%fused_computation.1 | loop fusion | flops 1048576 | bytes 8388610 | tf_op jit(solution)/shard_map/jit(_where)/select_n | solution.py:67
  113.1 7.7 %collective-permute-start.2 = (f32[2,512,512]{2,1,0:T(8,128)S(1)}, f32[2,512,512]{2,1,0:T(8,128)S(1)}, u32[]{:S(2)}, u32[]{:S(2)}) collective-permute-start(f32[2,512,512]{2,1,0:T(8,128)S(1)} %select_select_fusion.mine_ref), channel_id=1, source_target_pairs={{0,1},{1,0},{2,3},{3,2},{4,5},{5,4},{6,7},{7,6},{8,9},{9,8},{10,11... | collective-permute-start | bytes 6291464 | tf_op jit(solution)/shard_map/ppermute | solution.py:57
  128.4 7.7 %collective-permute-done.22 = f32[2048,128]{1,0:T(8,128)S(1)} collective-permute-done((f32[2048,128]{1,0:T(8,128)S(1)}, f32[2048,128]{1,0:T(8,128)S(1)}, u32[]{:S(2)}, u32[]{:S(2)}) %collective-permute-start.22) | collective-permute-done | bytes 1048608 | tf_op jit(solution)/shard_map/ppermute | solution.py:57
  136.2 2.3 %collective-permute-done.21 = f32[2048,128]{1,0:T(8,128)S(1)} collective-permute-done((f32[2048,128]{1,0:T(8,128)S(1)}, f32[2048,128]{1,0:T(8,128)S(1)}, u32[]{:S(2)}, u32[]{:S(2)}) %collective-permute-start.21) | collective-permute-done | bytes 1048608 | tf_op jit(solution)/shard_map/ppermute | solution.py:57
  141.2 18.8 %shard_map.43 = (f32[2,2,512,512]{3,2,1,0:T(8,128)}, bf16[4,1024,256]{2,1,0:T(8,128)(2,1)S(1)}, bf16[4,1024,256]{2,1,0:T(8,128)(2,1)}, bf16[4,1024,256]{2,1,0:T(8,128)(2,1)}, bf16[4,1024,256]{2,1,0:T(8,128)(2,1)}) custom-call(s32[3]{0:T(128)S(1)} %pad_add_fusion.where_ref, f32[2,512,512]{2,1,0:T(8,128)} %copy-done.1, f32[2,512,512]{2,1,0:T(8,128)} %copy-done.2, ...), custom_call_target="tpu_custom_call" | custom-call | flops 20000000000 | bytes 25165824 | tf_op jit(solution)/shard_map/pallas_call | solution.py:145
  160.0 22.2 %shard_map.44.x_ref = f32[16384,128]{1,0:T(8,128)} custom-call(s32[3]{0:T(128)S(1)} %bitcast.84, f32[16384,128]{1,0:T(8,128)} %bitcast.91, bf16[4,1024,256]{2,1,0:T(8,128)(2,1)S(1)} %get-tuple-element.8.yg_high, bf16[4,1024,256]{2,1,0:T(8,128)(2,1)} %get-tuple-element.9.yg_low, bf16[4,1024,256]{2,1,0:T(8,128)(2,1)} %get-tuple-element.10.ye_high, ...), custom_call_target="tpu_custom_call" | custom-call | flops 9900000256 | bytes 27262976 | tf_op jit(solution)/shard_map/pallas_call | solution.py:205
  182.2 14.3 %shard_map.45 = f32[16384,128]{1,0:T(8,128)} custom-call(s32[1]{0:T(128)} %slice.33.ks_ref, f32[16384,128]{1,0:T(8,128)} %shard_map.44.x_ref, bf16[4,1024,256]{2,1,0:T(8,128)(2,1)S(1)} %get-tuple-element.8.yg_high, bf16[4,1024,256]{2,1,0:T(8,128)(2,1)} %get-tuple-element.9.yg_low, bf16[4,1024,256]{2,1,0:T(8,128)(2,1)} %get-tuple-element.10.ye_high, ...), custom_call_target="tpu_custom_call" | custom-call | flops 3300000000 | bytes 23068672 | tf_op jit(solution)/shard_map/pallas_call | solution.py:205
  (62 shorter events, 33.9 us)
Async XLA Ops:
  4.4 14.0 %collective-permute-start.10 = (f32[2048,128]{1,0:T(8,128)}, f32[2048,128]{1,0:T(8,128)S(1)}, u32[]{:S(2)}, u32[]{:S(2)}) collective-permute-start(f32[2048,128]{1,0:T(8,128)} %get-tuple-element.18), channel_id=1, source_target_pairs={{0,8},{1,33},{2,10},{3,35},{4,12},{5,37},{6,14},{7,39},{8,16},{9,4... | collective-permute-start | bytes 3145736 | tf_op jit(solution)/shard_map/ppermute | solution.py:57
  5.1 13.3 %collective-permute-start.12 = (f32[2048,128]{1,0:T(8,128)}, f32[2048,128]{1,0:T(8,128)S(1)}, u32[]{:S(2)}, u32[]{:S(2)}) collective-permute-start(f32[2048,128]{1,0:T(8,128)} %get-tuple-element.19), channel_id=1, source_target_pairs={{0,24},{1,97},{2,26},{3,99},{4,28},{5,101},{6,30},{7,103},{8,0},{9... | collective-permute-start | bytes 3145736 | tf_op jit(solution)/shard_map/ppermute | solution.py:57
  5.8 12.5 %collective-permute-start.11 = (f32[2048,128]{1,0:T(8,128)}, f32[2048,128]{1,0:T(8,128)}, u32[]{:S(2)}, u32[]{:S(2)}) collective-permute-start(f32[2048,128]{1,0:T(8,128)} %get-tuple-element.20), channel_id=1, source_target_pairs={{0,16},{1,65},{2,18},{3,67},{4,20},{5,69},{6,22},{7,71},{8,24},{9,... | collective-permute-start | bytes 3145736 | tf_op jit(solution)/shard_map/ppermute | solution.py:57
  13.0 54.7 %collective-permute-start = (f32[2,512,512]{2,1,0:T(8,128)}, f32[2,512,512]{2,1,0:T(8,128)}, u32[]{:S(2)}, u32[]{:S(2)}) collective-permute-start(f32[2,512,512]{2,1,0:T(8,128)} %shard_map.41), channel_id=1, source_target_pairs={{0,2},{1,7},{8,10},{9,15},{16,18},{17,23},{24,26},{25,31},{32,34},... | collective-permute-start | bytes 6291464 | tf_op jit(solution)/shard_map/ppermute | solution.py:57
  17.5 9.1 %collective-permute-start.3 = (f32[256,512]{1,0:T(8,128)S(1)}, f32[256,512]{1,0:T(8,128)S(1)}, u32[]{:S(2)}, u32[]{:S(2)}) collective-permute-start(f32[256,512]{1,0:T(8,128)S(1)} %shard_map.42), channel_id=1, source_target_pairs={{0,2},{1,7},{8,10},{9,15},{16,18},{17,23},{24,26},{25,31},{32,34},... | collective-permute-start | bytes 1572872 | tf_op jit(solution)/shard_map/ppermute | solution.py:57
  20.8 7.2 %collective-permute-start.15 = (f32[2,512,128]{2,1,0:T(8,128)}, f32[2,512,128]{2,1,0:T(8,128)}, u32[]{:S(2)}, u32[]{:S(2)}) collective-permute-start(f32[2,512,128]{2,1,0:T(8,128)} %pad_maximum_fusion.4), channel_id=1, source_target_pairs={{0,96},{1,25},{2,98},{3,27},{4,100},{5,29},{6,102},{7,31},{8,104},... | collective-permute-start | bytes 1572872 | tf_op jit(solution)/shard_map/ppermute | solution.py:57
  23.1 21.6 %collective-permute-start.14 = (f32[2,512,128]{2,1,0:T(8,128)}, f32[2,512,128]{2,1,0:T(8,128)}, u32[]{:S(2)}, u32[]{:S(2)}) collective-permute-start(f32[2,512,128]{2,1,0:T(8,128)} %pad_maximum_fusion.3), channel_id=1, source_target_pairs={{0,64},{1,17},{2,66},{3,19},{4,68},{5,21},{6,70},{7,23},{8,72},{9,... | collective-permute-start | bytes 1572872 | tf_op jit(solution)/shard_map/ppermute | solution.py:57
  25.2 24.9 %collective-permute-start.13 = (f32[2,512,128]{2,1,0:T(8,128)}, f32[2,512,128]{2,1,0:T(8,128)}, u32[]{:S(2)}, u32[]{:S(2)}) collective-permute-start(f32[2,512,128]{2,1,0:T(8,128)} %pad_maximum_fusion.2), channel_id=1, source_target_pairs={{0,32},{1,9},{2,34},{3,11},{4,36},{5,13},{6,38},{7,15},{8,40},{9,1... | collective-permute-start | bytes 1572872 | tf_op jit(solution)/shard_map/ppermute | solution.py:57
  26.7 29.3 %collective-permute-start.4 = (f32[256,512]{1,0:T(8,128)S(1)}, f32[256,512]{1,0:T(8,128)S(1)}, u32[]{:S(2)}, u32[]{:S(2)}) collective-permute-start(f32[256,512]{1,0:T(8,128)S(1)} %broadcast_select_fusion.1), channel_id=1, source_target_pairs={{0,6},{1,3},{2,4},{7,5},{8,14},{9,11},{10,12},{15,13},{16,22},{17,... | collective-permute-start | bytes 1572872 | tf_op jit(solution)/shard_map/ppermute | solution.py:57
  53.2 19.2 %collective-permute-start.16 = (f32[2,512,128]{2,1,0:T(8,128)S(1)}, f32[2,512,128]{2,1,0:T(8,128)S(1)}, u32[]{:S(2)}, u32[]{:S(2)}) collective-permute-start(f32[2,512,128]{2,1,0:T(8,128)S(1)} %pad_maximum_fusion.5), channel_id=1, source_target_pairs={{0,32},{1,9},{2,34},{3,11},{4,36},{5,13},{6,38},{7,15},{8,40},{9,1... | collective-permute-start | bytes 1572872 | tf_op jit(solution)/shard_map/ppermute | solution.py:57
  56.1 11.6 %copy-start = (f32[2,512,512]{2,1,0:T(8,128)S(1)}, f32[2,512,512]{2,1,0:T(8,128)}, u32[]{:S(2)}) copy-start(f32[2,512,512]{2,1,0:T(8,128)} %shard_map.41) | copy-start | bytes 6291460
  56.1 22.0 %collective-permute-start.5 = (f32[256,512]{1,0:T(8,128)S(1)}, f32[256,512]{1,0:T(8,128)S(1)}, u32[]{:S(2)}, u32[]{:S(2)}) collective-permute-start(f32[256,512]{1,0:T(8,128)S(1)} %select_select_fusion.3), channel_id=1, source_target_pairs={{1,9},{3,11},{5,13},{7,15},{8,40},{10,42},{12,44},{14,46}} | collective-permute-start | bytes 1572872 | tf_op jit(solution)/shard_map/ppermute | solution.py:57
  57.0 18.2 %collective-permute-start.17 = (f32[2,512,128]{2,1,0:T(8,128)S(1)}, f32[2,512,128]{2,1,0:T(8,128)S(1)}, u32[]{:S(2)}, u32[]{:S(2)}) collective-permute-start(f32[2,512,128]{2,1,0:T(8,128)S(1)} %pad_maximum_fusion.5), channel_id=1, source_target_pairs={{0,96},{1,25},{2,98},{3,27},{4,100},{5,29},{6,102},{7,31},{8,104},... | collective-permute-start | bytes 1572872 | tf_op jit(solution)/shard_map/ppermute | solution.py:57
  63.4 13.9 %collective-permute-start.18 = (f32[2,512,128]{2,1,0:T(8,128)S(1)}, f32[2,512,128]{2,1,0:T(8,128)S(1)}, u32[]{:S(2)}, u32[]{:S(2)}) collective-permute-start(f32[2,512,128]{2,1,0:T(8,128)S(1)} %pad_maximum_fusion.5), channel_id=1, source_target_pairs={{0,64},{1,17},{2,66},{3,19},{4,68},{5,21},{6,70},{7,23},{8,72},{9,... | collective-permute-start | bytes 1572872 | tf_op jit(solution)/shard_map/ppermute | solution.py:57
  71.1 39.6 %collective-permute-start.1 = (f32[2,512,512]{2,1,0:T(8,128)}, f32[2,512,512]{2,1,0:T(8,128)}, u32[]{:S(2)}, u32[]{:S(2)}) collective-permute-start(f32[2,512,512]{2,1,0:T(8,128)} %broadcast_select_fusion), channel_id=1, source_target_pairs={{0,6},{1,3},{2,4},{7,5},{8,14},{9,11},{10,12},{15,13},{16,22},{17,... | collective-permute-start | bytes 6291464 | tf_op jit(solution)/shard_map/ppermute | solution.py:57
  78.2 42.7 %collective-permute-start.20 = (f32[2,2048,128]{2,1,0:T(8,128)}, f32[2,2048,128]{2,1,0:T(8,128)}, u32[]{:S(2)}, u32[]{:S(2)}) collective-permute-start(f32[2,2048,128]{2,1,0:T(8,128)} %bitcast.33), channel_id=1, source_target_pairs={{0,24},{1,97},{2,26},{3,99},{4,28},{5,101},{6,30},{7,103},{8,0},{9... | collective-permute-start | bytes 6291464 | tf_op jit(solution)/shard_map/ppermute | solution.py:57
  78.2 13.2 %collective-permute-start.6 = (f32[256,512]{1,0:T(8,128)S(1)}, f32[256,512]{1,0:T(8,128)S(1)}, u32[]{:S(2)}, u32[]{:S(2)}) collective-permute-start(f32[256,512]{1,0:T(8,128)S(1)} %broadcast_select_fusion.2), channel_id=1, source_target_pairs={{1,25},{3,27},{5,29},{7,31},{8,104},{9,17},{10,106},{11,19},{12,10... | collective-permute-start | bytes 1572872 | tf_op jit(solution)/shard_map/ppermute | solution.py:57
  79.5 42.7 %collective-permute-start.19 = (f32[2,2048,128]{2,1,0:T(8,128)}, f32[2,2048,128]{2,1,0:T(8,128)}, u32[]{:S(2)}, u32[]{:S(2)}) collective-permute-start(f32[2,2048,128]{2,1,0:T(8,128)} %bitcast.33), channel_id=1, source_target_pairs={{0,8},{1,33},{2,10},{3,35},{4,12},{5,37},{6,14},{7,39},{8,16},{9,4... | collective-permute-start | bytes 6291464 | tf_op jit(solution)/shard_map/ppermute | solution.py:57
  91.6 17.7 %collective-permute-start.7 = (f32[256,512]{1,0:T(8,128)S(1)}, f32[256,512]{1,0:T(8,128)S(1)}, u32[]{:S(2)}, u32[]{:S(2)}) collective-permute-start(f32[256,512]{1,0:T(8,128)S(1)} %select_select_fusion.2), channel_id=1, source_target_pairs={{1,33},{3,35},{5,37},{7,39},{8,16},{9,41},{10,18},{11,43},{12,20},... | collective-permute-start | bytes 1572872 | tf_op jit(solution)/shard_map/ppermute | solution.py:57
  109.4 15.7 %collective-permute-start.8 = (f32[256,512]{1,0:T(8,128)S(1)}, f32[256,512]{1,0:T(8,128)S(1)}, u32[]{:S(2)}, u32[]{:S(2)}) collective-permute-start(f32[256,512]{1,0:T(8,128)S(1)} %broadcast_select_fusion.3), channel_id=1, source_target_pairs={{1,97},{3,99},{5,101},{7,103},{8,0},{9,105},{10,2},{11,107},{12,4}... | collective-permute-start | bytes 1572872 | tf_op jit(solution)/shard_map/ppermute | solution.py:57
  113.1 26.8 %collective-permute-start.2 = (f32[2,512,512]{2,1,0:T(8,128)S(1)}, f32[2,512,512]{2,1,0:T(8,128)S(1)}, u32[]{:S(2)}, u32[]{:S(2)}) collective-permute-start(f32[2,512,512]{2,1,0:T(8,128)S(1)} %select_select_fusion.mine_ref), channel_id=1, source_target_pairs={{0,1},{1,0},{2,3},{3,2},{4,5},{5,4},{6,7},{7,6},{8,9},{9,8},{10,11... | collective-permute-start | bytes 6291464 | tf_op jit(solution)/shard_map/ppermute | solution.py:57
  122.1 14.0 %collective-permute-start.22 = (f32[2048,128]{1,0:T(8,128)S(1)}, f32[2048,128]{1,0:T(8,128)S(1)}, u32[]{:S(2)}, u32[]{:S(2)}) collective-permute-start(f32[2048,128]{1,0:T(8,128)S(1)} %slice_bitcast_fusion), channel_id=1, source_target_pairs={{0,24},{1,97},{2,26},{3,99},{4,28},{5,101},{6,30},{7,103},{8,0},{9... | collective-permute-start | bytes 3145736 | tf_op jit(solution)/shard_map/ppermute | solution.py:57
  123.5 14.9 %collective-permute-start.21 = (f32[2048,128]{1,0:T(8,128)S(1)}, f32[2048,128]{1,0:T(8,128)S(1)}, u32[]{:S(2)}, u32[]{:S(2)}) collective-permute-start(f32[2048,128]{1,0:T(8,128)S(1)} %slice_bitcast_fusion.1), channel_id=1, source_target_pairs={{0,8},{1,33},{2,10},{3,35},{4,12},{5,37},{6,14},{7,39},{8,16},{9,4... | collective-permute-start | bytes 3145736 | tf_op jit(solution)/shard_map/ppermute | solution.py:57
  125.2 3.0 %collective-permute-start.9 = (f32[256,512]{1,0:T(8,128)S(1)}, f32[256,512]{1,0:T(8,128)S(1)}, u32[]{:S(2)}, u32[]{:S(2)}) collective-permute-start(f32[256,512]{1,0:T(8,128)S(1)} %select_select_fusion.1), channel_id=1, source_target_pairs={{0,1},{1,0},{2,3},{3,2},{4,5},{5,4},{6,7},{7,6},{8,9},{9,8},{10,11... | collective-permute-start | bytes 1572872 | tf_op jit(solution)/shard_map/ppermute | solution.py:57
  (2 other events, 11.8 us)

commit v2 on v1

--- a/solution.py
+++ b/solution.py
@@ -10,9 +10,8 @@
 AXES = ("row", "col")
 RING = 4
 MOVES = (1, -1, 2)
+SPLIT = 2
 VMEM_BYTES = 50 * 1024 * 1024
-NN = (((1,), (0,)), ((), ()))
-NT = (((1,), (1,)), ((), ()))
 
 
 def place(z, y, x, c):
@@ -83,137 +82,168 @@
     return high, low
 
 
-def dot3(a, b, dims):
-    a_high, a_low = a
-    b_high, b_low = b
-    one = functools.partial(
-        lax.dot_general, dimension_numbers=dims, preferred_element_type=jnp.float32
-    )
-    return one(a_high, b_high) + (one(a_high, b_low) + one(a_low, b_high))
+def stack_left(x):
+    high, low = split(x)
+    return jnp.concatenate([high, high, low], axis=1)
+
+
+def put_right(ref, columns, x):
+    high, low = split(x)
+    depth = x.shape[0]
+    for i, value in enumerate((high, low, high)):
+        ref[i * depth : (i + 1) * depth, columns] = value
+
+
+def dot(a, b):
+    return jnp.dot(a, b, preferred_element_type=jnp.float32)
+
+
+def weights_kernel(inv_ref, first_ref, second_ref, right):
+    nb = inv_ref.shape[1]
+    for i, out_ref in enumerate((first_ref, second_ref)):
+        inv = inv_ref[i]
+        turned = inv.T
+        put_right(right, slice(None), inv)
+        put_right(out_ref, slice(0, nb), turned)
+        put_right(out_ref, slice(nb, 2 * nb), dot(stack_left(turned), right[...]))
+
+
+def weights(inverse_factors):
+    _, nb, _ = inverse_factors.shape
+    return pl.pallas_call(
+        weights_kernel,
+        out_shape=[jax.ShapeDtypeStruct((3 * nb, 2 * nb), jnp.bfloat16)] * 2,
+        scratch_shapes=[pltpu.VMEM((3 * nb, nb), jnp.bfloat16)],
+        compiler_params=pltpu.CompilerParams(vmem_limit_bytes=VMEM_BYTES),
+        cost_estimate=pl.CostEstimate(flops=2 * 10**9, bytes_accessed=8 * 2**20, transcendentals=0),
+    )(inverse_factors)
 
 
 def factors_kernel(
-    where_ref, mine_ref, theirs_ref, corner_ref, inv_ref,
+    where_ref, mine_ref, theirs_ref, corner_ref, first_ref, second_ref,
     panels_ref, yg_high, yg_low, ye_high, ye_low,
-    inv_high, inv_low, p01_high, p01_low, f_high, f_low,
+    f_turned, f_right,
 ):
     a = pl.program_id(0)
     prow, pcol, core = where_ref[0], where_ref[1], where_ref[2]
     part = yg_high.shape[2] // 2
+    nb = mine_ref.shape[2]
 
     @pl.when((a == 0) & (pl.program_id(1) == 0))
     def _():
-        for i in range(2):
-            inv_high[i], inv_low[i] = split(inv_ref[i])
-        inv0 = inv_high[0], inv_low[0]
-        p01 = split(dot3(split(corner_ref[...]), inv0, NT))
-        p01_high[...], p01_low[...] = p01
-        f_high[...], f_low[...] = split(dot3(p01, inv0, NN))
-
-    inv0 = inv_high[0], inv_low[0]
-    inv1 = inv_high[1], inv_low[1]
+        f = dot(stack_left(corner_ref[...]), first_ref[:, nb:])
+        put_right(f_right, slice(None), f)
+        put_right(f_turned, slice(None), f.T)
+
     mine, theirs = mine_ref[0], theirs_ref[0]
-    left = jnp.where(core == 0, mine, theirs)
+    left = stack_left(jnp.where(core == 0, mine, theirs))
     right = jnp.where(core == 0, theirs, mine)
     block = a * 16 + prow
-    p0 = dot3(split(left), inv0, NT)
-    p0_parts = split(p0)
-    below = right - dot3(p0_parts, (p01_high[...], p01_low[...]), NT)
-    p1 = jnp.where(block >= 1, dot3(split(below), inv1, NT), 0.0)
-    panels_ref[0, 0] = p0
-    panels_ref[1, 0] = p1
-    z0 = jnp.where(block >= 1, dot3(p0_parts, inv0, NN), 0.0)
-    y1 = jnp.where(block >= 2, dot3(split(p1), inv1, NN), 0.0)
-    y0 = z0 - dot3(split(y1), (f_high[...], f_low[...]), NN)
+    panels_ref[0, 0] = dot(left, first_ref[:, :nb])
+    z0 = jnp.where(block >= 1, dot(left, first_ref[:, nb:]), 0.0)
+    below = stack_left(right - dot(left, f_turned[...]))
+    panels_ref[1, 0] = jnp.where(block >= 1, dot(below, second_ref[:, :nb]), 0.0)
+    y1 = jnp.where(block >= 2, dot(below, second_ref[:, nb:]), 0.0)
+    y0 = z0 - dot(stack_left(y1), f_right[...])
     e0 = jnp.where(pcol == 0, 0.0, jnp.where(pcol == 1, z0, y0))
     e1 = jnp.where(pcol <= 1, 0.0, y1)
     for high, low, first, second in ((yg_high, yg_low, y0, y1), (ye_high, ye_low, e0, e1)):
-        for k in range(RING):
-            for i, value in enumerate((first, second)):
-                h, l = split(value[:, k * part : (k + 1) * part])
-                high[k, :, i * part : (i + 1) * part] = h
-                low[k, :, i * part : (i + 1) * part] = l
-
-
-def row_factors(where, mine, theirs, corner, inverse_factors):
+        for i, value in enumerate((first, second)):
+            h, l = split(value)
+            for k in range(RING):
+                high[k, :, i * part : (i + 1) * part] = h[:, k * part : (k + 1) * part]
+                low[k, :, i * part : (i + 1) * part] = l[:, k * part : (k + 1) * part]
+
+
+def row_factors(where, mine, theirs, corner, first, second):
     rbd, nb, _ = mine.shape
-    tile = nb // 2
+    tile = nb // SPLIT
     rows = pl.BlockSpec((1, tile, nb), lambda a, t: (a, t, 0))
-    parts = pl.BlockSpec((RING, tile, nb // 2), lambda a, t: (0, a * 2 + t, 0))
+    parts = pl.BlockSpec((RING, tile, nb // 2), lambda a, t: (0, a * SPLIT + t, 0))
     parts_shape = jax.ShapeDtypeStruct((RING, rbd * nb, nb // 2), jnp.bfloat16)
-    half = pltpu.VMEM((nb, nb), jnp.bfloat16)
+    fixed = [
+        pl.BlockSpec(x.shape, lambda a, t: (0, 0), pipeline_mode=pl.Buffered(buffer_count=1))
+        for x in (corner, first, second)
+    ]
     return pl.pallas_call(
         factors_kernel,
-        grid=(rbd, 2),
-        in_specs=[
-            pl.BlockSpec(memory_space=pltpu.SMEM),
-            rows,
-            rows,
-            pl.BlockSpec((nb, nb), lambda a, t: (0, 0)),
-            pl.BlockSpec((2, nb, nb), lambda a, t: (0, 0, 0)),
-        ],
+        grid=(rbd, SPLIT),
+        in_specs=[pl.BlockSpec(memory_space=pltpu.SMEM), rows, rows] + fixed,
         out_specs=[pl.BlockSpec((2, 1, tile, nb), lambda a, t: (0, a, t, 0))] + [parts] * 4,
         out_shape=[jax.ShapeDtypeStruct((2, rbd, nb, nb), jnp.float32)] + [parts_shape] * 4,
-        scratch_shapes=[pltpu.VMEM((2, nb, nb), jnp.bfloat16)] * 2 + [half] * 4,
+        scratch_shapes=[pltpu.VMEM((3 * nb, nb), jnp.bfloat16)] * 2,
         compiler_params=pltpu.CompilerParams(vmem_limit_bytes=VMEM_BYTES),
-        cost_estimate=pl.CostEstimate(flops=20 * 10**9, bytes_accessed=24 * 2**20, transcendentals=0),
-    )(where, mine, theirs, corner, inverse_factors)
-
-
-def update_kernel(count, ks_ref, x_ref, yg_high, yg_low, ye_high, ye_low, *rest):
-    pieces, out_ref, rhs = rest[:count], rest[count], rest[count + 1]
-    rows = yg_high.shape[1]
-    depth = yg_high.shape[2]
+        cost_estimate=pl.CostEstimate(flops=11 * 10**9, bytes_accessed=24 * 2**20, transcendentals=0),
+    )(where, mine, theirs, corner, first, second)
+
+
+def update_kernel(count, ks_ref, x_ref, *rest):
+    factors, halves = rest[: 4 * count], rest[4 * count : 6 * count]
+    out_ref, rhs = rest[6 * count], rest[6 * count + 1]
+    rows, depth = factors[0].shape[1:]
+    half = depth // 2
     cbd = rhs.shape[0]
     lanes = rhs.shape[2] // RING
     stride = RING * cbd
 
     @pl.when((pl.program_id(0) == 0) & (pl.program_id(1) == 0))
     def _():
-        for j in range(count):
+        for j in range(2 * count):
             for c in range(cbd):
                 for t in range(RING):
-                    high, low = split(pieces[j][pl.ds(t * cbd + c, depth, stride=stride), :])
+                    high, low = split(halves[j][pl.ds(t * cbd + c, half, stride=stride), :])
                     for place_at, value in ((0, high), (1, low), (2, high)):
-                        start = (3 * j + place_at) * depth
-                        rhs[c, start : start + depth, t * lanes : (t + 1) * lanes] = value
+                        start = (3 * (j // 2) + place_at) * depth + (j % 2) * half
+                        rhs[c, start : start + half, t * lanes : (t + 1) * lanes] = value
 
     left = []
-    for high, low in ((ye_high, ye_low), (yg_high, yg_low)):
+    for kind in (1, 0):
         terms = []
         for j in range(count):
-            h, l = high[ks_ref[j]], low[ks_ref[j]]
+            h, l = factors[4 * j + 2 * kind][0], factors[4 * j + 2 * kind + 1][0]
             terms += [h, h, l]
         left.append(jnp.concatenate(terms, axis=1))
     for c in range(cbd):
-        product = jnp.dot(left[min(c, 1)], rhs[c], preferred_element_type=jnp.float32)
+        product = dot(left[min(c, 1)], rhs[c])
         for t in range(RING):
             at = pl.ds(t * cbd + c, rows, stride=stride)
             out_ref[at, :] = x_ref[at, :] - product[:, t * lanes : (t + 1) * lanes]
 
 
-def subtract_products(lines, factors, ks, pieces, cbd):
+def subtract_products(lines, factors, ks, halves, cbd):
     nb = 2 * factors[0].shape[2]
     rbd = factors[0].shape[1] // nb
-    count = len(pieces)
-    tile = nb // 2
-    block = pl.BlockSpec((tile * RING * cbd, lines.shape[1]), lambda a, t: (a * 2 + t, 0))
-    parts = pl.BlockSpec((RING, tile, nb // 2), lambda a, t: (0, a * 2 + t, 0))
-    whole = pl.BlockSpec(
-        pieces[0].shape, lambda a, t: (0, 0), pipeline_mode=pl.Buffered(buffer_count=1)
-    )
+    count = len(halves) // 2
+    tile = nb // SPLIT
+    block = pl.BlockSpec((tile * RING * cbd, lines.shape[1]), lambda a, t, ks: (a * SPLIT + t, 0))
+    parts = [
+        pl.BlockSpec((1, tile, nb // 2), lambda a, t, ks, j=j: (ks[j], a * SPLIT + t, 0))
+        for j in range(count)
+        for _ in factors
+    ]
+    whole = [
+        pl.BlockSpec(
+            (nb // RING * RING * cbd, lines.shape[1]),
+            lambda a, t, ks, i=i: (i, 0),
+            pipeline_mode=pl.Buffered(buffer_count=1),
+        )
+        for _, i in halves
+    ]
     return pl.pallas_call(
         functools.partial(update_kernel, count),
-        grid=(rbd, 2),
-        in_specs=[pl.BlockSpec(memory_space=pltpu.SMEM), block] + [parts] * 4 + [whole] * count,
-        out_specs=block,
+        grid_spec=pltpu.PrefetchScalarGridSpec(
+            num_scalar_prefetch=1,
+            grid=(rbd, SPLIT),
+            in_specs=[block] + parts + whole,
+            out_specs=block,
+            scratch_shapes=[pltpu.VMEM((cbd, 3 * count * (nb // 2), nb), jnp.bfloat16)],
+        ),
         out_shape=jax.ShapeDtypeStruct(lines.shape, lines.dtype),
-        scratch_shapes=[pltpu.VMEM((cbd, 3 * count * (nb // 2), nb), jnp.bfloat16)],
         compiler_params=pltpu.CompilerParams(vmem_limit_bytes=VMEM_BYTES),
         cost_estimate=pl.CostEstimate(
-            flops=3 * count * 11 * 10**8, bytes_accessed=(16 + 4 + 2 * count) * 2**20, transcendentals=0
+            flops=3 * count * 11 * 10**8, bytes_accessed=(16 + 4 * count) * 2**20, transcendentals=0
         ),
-    )(ks, lines, *factors, *pieces)
+    )(ks, lines, *(factors * count), *(t for t, _ in halves))
 
 
 def column_kernel(x_ref, out_ref):
@@ -324,11 +354,7 @@
 
     before = send(whole, along_u(1))
     after = send(whole, along_u(-1))
-    far_a = send(before[0], along_u(1))
-    far_b = send(after[1], along_u(-1))
-    far = jnp.concatenate([far_a, far_b])
-    lanes = lines.shape[1]
-    return [t.reshape(-1, lanes) for t in (whole, before, after, far)]
+    return whole, before, after
 
 
 def row_inputs(column, start, u, v, x, c):
@@ -346,8 +372,6 @@
     s = jnp.where(c == 0, x, -x) % RING
     start = share(start, s, pairs(x_first), pairs(x_second))
     mine = share(column, s, pairs(x_first), pairs(x_second))
-    theirs = other_core(mine)
-
     def uv(z, y, c):
         return (y, z) if c == 0 else (z, y)
 
@@ -375,7 +399,7 @@
     here = share(line, (u - 1 + c) % RING, pairs(u_first), pairs(u_second))
     there = other_core(here)
     corner = jnp.concatenate([jnp.where(c == 0, here, there), jnp.where(c == 0, there, here)])
-    return mine, theirs, corner
+    return mine, corner
 
 
 def body(matrix, inverse_factors):
@@ -388,15 +412,22 @@
     v = jnp.where(c == 0, z, y)
 
     lines = to_lines(matrix)
-    own, before, after, far = top_rows(lines, u, v, c)
+    own, before, after = top_rows(lines, u, v, c)
     start = corner_half(c.astype(jnp.int32)[None], lines, nb, cbd)
-    mine, theirs, corner = row_inputs(first_column(lines, rbd, nb, cbd), start, u, v, x, c)
+    mine, corner = row_inputs(first_column(lines, rbd, nb, cbd), start, u, v, x, c)
+    before, after, mine, turned = lax.optimization_barrier(
+        (before, after, mine, weights(inverse_factors))
+    )
+    far = send(before[0], along_u(1)), send(after[1], along_u(-1))
+    theirs = other_core(mine)
 
     where = jnp.stack([prow, pcol, c]).astype(jnp.int32)
-    panels, *factors = row_factors(where, mine, theirs, corner, inverse_factors)
+    panels, *factors = row_factors(where, mine, theirs, corner, *turned)
     ks = jnp.stack([u, u - 1, u + 1, u + 2]).astype(jnp.int32) % RING
-    partial = subtract_products(lines, factors, ks[:3], (own, before, after), cbd)
-    final = subtract_products(partial, factors, ks[3:], (far,), cbd)
+    far, factors = lax.optimization_barrier((far, factors))
+    halves = [(t.reshape(-1, lines.shape[1]), i) for t in (own, before, after) for i in range(2)]
+    halves += [(t, 0) for t in far]
+    final = subtract_products(lines, factors, ks, halves, cbd)
     return panels, from_lines(final, matrix.shape)
 
 

time: 199 us -> 179 us (0.90)
  waiting for transfers between devices: 66.2 us -> 49.6 us
  Pallas kernels: 63.3 us -> 58.3 us
    ppermute x23, waiting for transfers between devices: 66.2 us -> 49.6 us  [send(): return lax.ppermute(x, AXES, moves)]
    pallas_call x3, Pallas kernels: 55.2 us -> 50.2 us  [the longest x1 27.6 us: subtract_products(): pl.pallas_call(functools.partial(update_kernel, count), grid_spec=pltpu.P...]
    select_n x4, other arithmetic: 2.81 us -> 4.87 us  [choose(): result = jnp.where(index == i, options[i], result)]
  transfers between devices with their start and end apart: 23 -> 23, of which waited for: 10 -> 7; matrix products, arithmetic and copies ran while one was open for 12% -> 14% of each run, Pallas kernels for 4% -> 17%
where the time goes in v2:
time: 179 us; the launch traced here: 176 us
  Pallas kernels  58.3 us (33%)
  waiting for transfers between devices  49.6 us (28%)
  starting transfers between devices  35.6 us (20%)
  other arithmetic  17.9 us (10%)
  local copies, waits for them, and re-layouts  13 us (7%)
    ppermute x23, waiting for transfers between devices, send(): return lax.ppermute(x, AXES, moves)  49.6 us
    ppermute x23, starting transfers between devices, send(): return lax.ppermute(x, AXES, moves)  35.6 us
    pallas_call x1, Pallas kernels, subtract_products(): pl.pallas_call(functools.partial(update_kernel, count), grid_spec=pltpu.P...  27.6 us
    pallas_call x1, Pallas kernels, row_factors(): pl.pallas_call(factors_kernel, grid=(rbd, SPLIT), in_specs=[pl.BlockSpec(...  18.6 us
    pallas_call x1, Pallas kernels, first_column(): pl.pallas_call(column_kernel, grid=(rbd, 2), in_specs=[pl.BlockSpec((tile...  5.56 us
    select_n x4, other arithmetic, choose(): result = jnp.where(index == i, options[i], result)  4.87 us
    another operation x4, other arithmetic, quarter(): return jnp.stack([choose(u, o, p, q, m), choose(u, m, o, p, q)])  4.59 us
    pallas_call x1, Pallas kernels, weights(): pl.pallas_call(weights_kernel, out_shape=[jax.ShapeDtypeStruct((3 * nb, 2...  4.04 us
  transfers between devices with their start and end apart: 23, of which 7 were waited for; matrix products, arithmetic and copies ran while one was open for 14% of the time, Pallas kernels for 17%

profile of v2, /device:TPU:21, one launch (start us, length us, event | category | flops | bytes accessed | tf_op | source)
XLA Modules:
  0.0 175.7 jit_solution(14946364226274729396)
XLA Ops:
  0.7 3.6 %constant_dynamic-slice_fusion.2 = (f32[2048,128]{1,0:T(8,128)}, f32[2048,128]{1,0:T(8,128)}, f32[2048,128]{1,0:T(8,128)}) fusion(f32[16384,128]{1,0:T(8,128)} %bitcast.83, s32[]{:T(128)S(6)} %select_n.400, s32[]{:T(128)S(6)} %select_n.405, s32[]{:T(128)S(6)} %select_n.403), kind=kLoop, calls=%fused_computation.40 | loop fusion | bytes 6291468 | tf_op jit(solution)/shard_map/dynamic_slice | solution.py:326
  4.4 1.6 collective-permute-start
  6.0 1.6 collective-permute-start.1
  7.7 1.6 collective-permute-start.2
  9.3 2.5 %shard_map.43 = f32[256,512]{1,0:T(8,128)S(1)} custom-call(s32[1]{0:T(128)} %bitcast.2.core_ref, f32[16384,128]{1,0:T(8,128)} %bitcast.84), custom_call_target="tpu_custom_call" | custom-call | bytes 5242880 | tf_op jit(solution)/shard_map/pallas_call | solution.py:289
  12.5 5.6 %shard_map.41 = f32[2,512,512]{2,1,0:T(8,128)} custom-call(f32[16384,128]{1,0:T(8,128)} %bitcast.85), custom_call_target="tpu_custom_call" | custom-call | bytes 10485760 | tf_op jit(solution)/shard_map/pallas_call | solution.py:260
  21.2 2.1 %select_bitcast_fusion.6 = (f32[1,512,128]{2,1,0:T(8,128)S(1)}, f32[1,512,128]{2,1,0:T(8,128)S(1)}, f32[1,512,128]{2,1,0:T(8,128)S(1)}, f32[1,512,128]{2,1,0:T(8...) fusion(f32[2048,128]{1,0:T(8,128)} %collective-permute-done.2, s32[]{:T(128)S(6)} %select_n.411, ...), kind=kLoop, calls=%fused_computation.31 | loop fusion | flops 1179648 | bytes 4718619 | tf_op jit(solution)/shard_map/stack | solution.py:339
  29.8 3.3 %collective-permute-done.15 = f32[256,512]{1,0:T(8,128)} collective-permute-done((f32[256,512]{1,0:T(8,128)}, f32[256,512]{1,0:T(8,128)}, u32[]{:S(2)}, u32[]{:S(2)}) %collective-permute-start.15) | collective-permute-done | bytes 524320 | tf_op jit(solution)/shard_map/ppermute | solution.py:56
  35.0 8.0 %collective-permute-done.3 = f32[2,512,128]{2,1,0:T(8,128)} collective-permute-done((f32[2,512,128]{2,1,0:T(8,128)}, f32[2,512,128]{2,1,0:T(8,128)}, u32[]{:S(2)}, u32[]{:S(2)}) %collective-permute-start.3) | collective-permute-done | bytes 524320 | tf_op jit(solution)/shard_map/ppermute | solution.py:56
  43.0 6.8 %collective-permute-done.4 = f32[2,512,128]{2,1,0:T(8,128)} collective-permute-done((f32[2,512,128]{2,1,0:T(8,128)}, f32[2,512,128]{2,1,0:T(8,128)}, u32[]{:S(2)}, u32[]{:S(2)}) %collective-permute-start.4) | collective-permute-done | bytes 524320 | tf_op jit(solution)/shard_map/ppermute | solution.py:56
  51.4 1.8 %fusion.4 = f32[1,512,128]{2,1,0:T(8,128)S(1)} fusion(f32[2,512,128]{2,1,0:T(8,128)} %collective-permute-done.5, f32[2,512,128]{2,1,0:T(8,128)} %collective-permute-done.4, f32[2,512,128]{2,1,0:T(8,128)} %collective-permute-done.3, f32[2048,128]{1,0:T(8,128)} %collective-permute-done.2, s32[]{:T(128)S(6)} %select_n.393, ...), kind=kLoop, calls=%fused_computation.21 | loop fusion | flops 851968 | bytes 2889216 | tf_op jit(solution)/shard_map/stack | solution.py:352
  53.2 2.8 %collective-permute-start.6 = (f32[2,512,128]{2,1,0:T(8,128)S(1)}, f32[2,512,128]{2,1,0:T(8,128)S(1)}, u32[]{:S(2)}, u32[]{:S(2)}) collective-permute-start(f32[2,512,128]{2,1,0:T(8,128)S(1)} %pad_maximum_fusion.4), channel_id=1, source_target_pairs={{0,32},{1,9},{2,34},{3,11},{4,36},{5,13},{6,38},{7,15},{8,40},{9,1... | collective-permute-start | bytes 1572872 | tf_op jit(solution)/shard_map/ppermute | solution.py:56
  56.0 2.2 %collective-permute-start.8 = (f32[2,512,128]{2,1,0:T(8,128)S(1)}, f32[2,512,128]{2,1,0:T(8,128)S(1)}, u32[]{:S(2)}, u32[]{:S(2)}) collective-permute-start(f32[2,512,128]{2,1,0:T(8,128)S(1)} %pad_maximum_fusion.4), channel_id=1, source_target_pairs={{0,64},{1,17},{2,66},{3,19},{4,68},{5,21},{6,70},{7,23},{8,72},{9,... | collective-permute-start | bytes 1572872 | tf_op jit(solution)/shard_map/ppermute | solution.py:56
  62.0 2.0 %broadcast_select_fusion = f32[2,512,512]{2,1,0:T(8,128)} fusion(f32[2,512,512]{2,1,0:T(8,128)S(1)} %copy-done.2, f32[2,512,512]{2,1,0:T(8,128)S(1)} %collective-permute-done.11, pred[]{:T(512)S(6)} %eq.47), kind=kLoop, calls=%fused_computation.4 | loop fusion | flops 524288 | bytes 6291457 | tf_op jit(solution)/shard_map/jit(_where)/select_n | solution.py:317
  70.4 3.4 %collective-permute-done.17 = f32[256,512]{1,0:T(8,128)S(1)} collective-permute-done((f32[256,512]{1,0:T(8,128)S(1)}, f32[256,512]{1,0:T(8,128)S(1)}, u32[]{:S(2)}, u32[]{:S(2)}) %collective-permute-start.17) | collective-permute-done | bytes 524320 | tf_op jit(solution)/shard_map/ppermute | solution.py:56
  75.3 23.9 %collective-permute-done.18 = f32[256,512]{1,0:T(8,128)S(1)} collective-permute-done((f32[256,512]{1,0:T(8,128)S(1)}, f32[256,512]{1,0:T(8,128)S(1)}, u32[]{:S(2)}, u32[]{:S(2)}) %collective-permute-start.18) | collective-permute-done | bytes 524320 | tf_op jit(solution)/shard_map/ppermute | solution.py:56
  100.1 2.1 %collective-permute-start.19 = (f32[256,512]{1,0:T(8,128)}, f32[256,512]{1,0:T(8,128)}, u32[]{:S(2)}, u32[]{:S(2)}) collective-permute-start(f32[256,512]{1,0:T(8,128)} %broadcast_select_fusion.3), channel_id=1, source_target_pairs={{1,97},{3,99},{5,101},{7,103},{8,0},{9,105},{10,2},{11,107},{12,4}... | collective-permute-start | bytes 1572872 | tf_op jit(solution)/shard_map/ppermute | solution.py:56
  102.2 4.0 %shard_map.42 = (bf16[1536,1024]{1,0:T(8,128)(2,1)}, bf16[1536,1024]{1,0:T(8,128)(2,1)}) custom-call(f32[2,512,512]{2,1,0:T(8,128)S(1)} %copy-done.1), custom_call_target="tpu_custom_call" | custom-call | flops 2000000000 | bytes 8388608 | tf_op jit(solution)/shard_map/pallas_call | solution.py:113
  106.3 2.3 %select_select_fusion.mine_ref = f32[2,512,512]{2,1,0:T(8,128)S(1)} fusion(f32[2,512,512]{2,1,0:T(8,128)} %shard_map.41, f32[2,512,512]{2,1,0:T(8,128)} %copy-done.3, f32[2,512,512]{2,1,0:T(8,128)} %collective-permute-done.12, pred[]{:T(512)S(6)} %eq.48, pred[]{:T(512)S(6)} %eq.47), kind=kLoop, calls=%fused_computation | loop fusion | flops 1048576 | bytes 8388610 | tf_op jit(solution)/shard_map/jit(_where)/select_n | solution.py:66
  108.7 7.7 %collective-permute-start.13 = (f32[2,512,512]{2,1,0:T(8,128)S(1)}, f32[2,512,512]{2,1,0:T(8,128)S(1)}, u32[]{:S(2)}, u32[]{:S(2)}) collective-permute-start(f32[2,512,512]{2,1,0:T(8,128)S(1)} %select_select_fusion.mine_ref), channel_id=1, source_target_pairs={{0,1},{1,0},{2,3},{3,2},{4,5},{5,4},{6,7},{7,6},{8,9},{9,8},{10,11... | collective-permute-start | bytes 6291464 | tf_op jit(solution)/shard_map/ppermute | solution.py:56
  117.8 3.1 %collective-permute-done.20 = f32[256,512]{1,0:T(8,128)S(1)} collective-permute-done((f32[256,512]{1,0:T(8,128)S(1)}, f32[256,512]{1,0:T(8,128)S(1)}, u32[]{:S(2)}, u32[]{:S(2)}) %collective-permute-start.20) | collective-permute-done | bytes 524320 | tf_op jit(solution)/shard_map/ppermute | solution.py:56
  124.8 1.8 collective-permute-start.22
  128.0 18.6 %shard_map.44 = (f32[2,2,512,512]{3,2,1,0:T(8,128)}, bf16[4,1024,256]{2,1,0:T(8,128)(2,1)S(1)}, bf16[4,1024,256]{2,1,0:T(8,128)(2,1)}, bf16[4,1024,256]{2,1,0:T(8,128)(2,1)}, bf16[4,1024,256]{2,1,0:T(8,128)(2,1)}) custom-call(s32[3]{0:T(128)S(1)} %pad_add_fusion.where_ref, f32[2,512,512]{2,1,0:T(8,128)} %copy-done.4, f32[2,512,512]{2,1,0:T(8,128)} %copy-done.5, ...), custom_call_target="tpu_custom_call" | custom-call | flops 11000000512 | bytes 25165824 | tf_op jit(solution)/shard_map/pallas_call | solution.py:168
  148.0 27.6 %shard_map.45 = f32[16384,128]{1,0:T(8,128)} custom-call(s32[4]{0:T(128)S(1)} %and_select_fusion.ks_ref, f32[16384,128]{1,0:T(8,128)} %bitcast.89, bf16[4,1024,256]{2,1,0:T(8,128)(2,1)} %copy-done, bf16[4,1024,256]{2,1,0:T(8,128)(2,1)} %get-tuple-element.33.rest_1_.rest_5_.rest_9_.rest_13_, ...), custom_call_target="tpu_custom_call" | custom-call | flops 13200000000 | bytes 33554432 | tf_op jit(solution)/shard_map/pallas_call | solution.py:232
  (66 shorter events, 34.2 us)
Async XLA Ops:
  4.4 16.8 %collective-permute-start = (f32[2048,128]{1,0:T(8,128)}, f32[2048,128]{1,0:T(8,128)}, u32[]{:S(2)}, u32[]{:S(2)}) collective-permute-start(f32[2048,128]{1,0:T(8,128)} %get-tuple-element.44), channel_id=1, source_target_pairs={{0,8},{1,33},{2,10},{3,35},{4,12},{5,37},{6,14},{7,39},{8,16},{9,4... | collective-permute-start | bytes 3145736 | tf_op jit(solution)/shard_map/ppermute | solution.py:56
  6.0 15.2 %collective-permute-start.1 = (f32[2048,128]{1,0:T(8,128)}, f32[2048,128]{1,0:T(8,128)}, u32[]{:S(2)}, u32[]{:S(2)}) collective-permute-start(f32[2048,128]{1,0:T(8,128)} %get-tuple-element.46), channel_id=1, source_target_pairs={{0,16},{1,65},{2,18},{3,67},{4,20},{5,69},{6,22},{7,71},{8,24},{9,... | collective-permute-start | bytes 3145736 | tf_op jit(solution)/shard_map/ppermute | solution.py:56
  7.7 13.5 %collective-permute-start.2 = (f32[2048,128]{1,0:T(8,128)}, f32[2048,128]{1,0:T(8,128)}, u32[]{:S(2)}, u32[]{:S(2)}) collective-permute-start(f32[2048,128]{1,0:T(8,128)} %get-tuple-element.45), channel_id=1, source_target_pairs={{0,24},{1,97},{2,26},{3,99},{4,28},{5,101},{6,30},{7,103},{8,0},{9... | collective-permute-start | bytes 3145736 | tf_op jit(solution)/shard_map/ppermute | solution.py:56
  11.8 7.2 %collective-permute-start.14 = (f32[256,512]{1,0:T(8,128)S(1)}, f32[256,512]{1,0:T(8,128)S(1)}, u32[]{:S(2)}, u32[]{:S(2)}) collective-permute-start(f32[256,512]{1,0:T(8,128)S(1)} %shard_map.43), channel_id=1, source_target_pairs={{0,2},{1,7},{8,10},{9,15},{16,18},{17,23},{24,26},{25,31},{32,34},... | collective-permute-start | bytes 1572872 | tf_op jit(solution)/shard_map/ppermute | solution.py:56
  18.0 43.9 %collective-permute-start.11 = (f32[2,512,512]{2,1,0:T(8,128)}, f32[2,512,512]{2,1,0:T(8,128)S(1)}, u32[]{:S(2)}, u32[]{:S(2)}) collective-permute-start(f32[2,512,512]{2,1,0:T(8,128)} %shard_map.41), channel_id=1, source_target_pairs={{0,2},{1,7},{8,10},{9,15},{16,18},{17,23},{24,26},{25,31},{32,34},... | collective-permute-start | bytes 6291464 | tf_op jit(solution)/shard_map/ppermute | solution.py:56
  19.9 13.2 %collective-permute-start.15 = (f32[256,512]{1,0:T(8,128)}, f32[256,512]{1,0:T(8,128)}, u32[]{:S(2)}, u32[]{:S(2)}) collective-permute-start(f32[256,512]{1,0:T(8,128)} %broadcast_select_fusion.1), channel_id=1, source_target_pairs={{0,6},{1,3},{2,4},{7,5},{8,14},{9,11},{10,12},{15,13},{16,22},{17,... | collective-permute-start | bytes 1572872 | tf_op jit(solution)/shard_map/ppermute | solution.py:56
  24.1 18.9 %collective-permute-start.3 = (f32[2,512,128]{2,1,0:T(8,128)}, f32[2,512,128]{2,1,0:T(8,128)}, u32[]{:S(2)}, u32[]{:S(2)}) collective-permute-start(f32[2,512,128]{2,1,0:T(8,128)} %pad_maximum_fusion.1), channel_id=1, source_target_pairs={{0,32},{1,9},{2,34},{3,11},{4,36},{5,13},{6,38},{7,15},{8,40},{9,1... | collective-permute-start | bytes 1572872 | tf_op jit(solution)/shard_map/ppermute | solution.py:56
  26.3 23.6 %collective-permute-start.4 = (f32[2,512,128]{2,1,0:T(8,128)}, f32[2,512,128]{2,1,0:T(8,128)}, u32[]{:S(2)}, u32[]{:S(2)}) collective-permute-start(f32[2,512,128]{2,1,0:T(8,128)} %pad_maximum_fusion.2), channel_id=1, source_target_pairs={{0,64},{1,17},{2,66},{3,19},{4,68},{5,21},{6,70},{7,23},{8,72},{9,... | collective-permute-start | bytes 1572872 | tf_op jit(solution)/shard_map/ppermute | solution.py:56
  28.4 21.5 %collective-permute-start.5 = (f32[2,512,128]{2,1,0:T(8,128)}, f32[2,512,128]{2,1,0:T(8,128)}, u32[]{:S(2)}, u32[]{:S(2)}) collective-permute-start(f32[2,512,128]{2,1,0:T(8,128)} %pad_maximum_fusion.3), channel_id=1, source_target_pairs={{0,96},{1,25},{2,98},{3,27},{4,100},{5,29},{6,102},{7,31},{8,104},... | collective-permute-start | bytes 1572872 | tf_op jit(solution)/shard_map/ppermute | solution.py:56
  34.3 24.0 %collective-permute-start.16 = (f32[256,512]{1,0:T(8,128)S(1)}, f32[256,512]{1,0:T(8,128)S(1)}, u32[]{:S(2)}, u32[]{:S(2)}) collective-permute-start(f32[256,512]{1,0:T(8,128)S(1)} %select_select_fusion.3), channel_id=1, source_target_pairs={{1,9},{3,11},{5,13},{7,15},{8,40},{10,42},{12,44},{14,46}} | collective-permute-start | bytes 1572872 | tf_op jit(solution)/shard_map/ppermute | solution.py:56
  53.2 12.1 %collective-permute-start.6 = (f32[2,512,128]{2,1,0:T(8,128)S(1)}, f32[2,512,128]{2,1,0:T(8,128)S(1)}, u32[]{:S(2)}, u32[]{:S(2)}) collective-permute-start(f32[2,512,128]{2,1,0:T(8,128)S(1)} %pad_maximum_fusion.4), channel_id=1, source_target_pairs={{0,32},{1,9},{2,34},{3,11},{4,36},{5,13},{6,38},{7,15},{8,40},{9,1... | collective-permute-start | bytes 1572872 | tf_op jit(solution)/shard_map/ppermute | solution.py:56
  56.0 10.2 %collective-permute-start.7 = (f32[2,512,128]{2,1,0:T(8,128)S(1)}, f32[2,512,128]{2,1,0:T(8,128)S(1)}, u32[]{:S(2)}, u32[]{:S(2)}) collective-permute-start(f32[2,512,128]{2,1,0:T(8,128)S(1)} %pad_maximum_fusion.4), channel_id=1, source_target_pairs={{0,96},{1,25},{2,98},{3,27},{4,100},{5,29},{6,102},{7,31},{8,104},... | collective-permute-start | bytes 1572872 | tf_op jit(solution)/shard_map/ppermute | solution.py:56
  56.0 12.1 %collective-permute-start.8 = (f32[2,512,128]{2,1,0:T(8,128)S(1)}, f32[2,512,128]{2,1,0:T(8,128)S(1)}, u32[]{:S(2)}, u32[]{:S(2)}) collective-permute-start(f32[2,512,128]{2,1,0:T(8,128)S(1)} %pad_maximum_fusion.4), channel_id=1, source_target_pairs={{0,64},{1,17},{2,66},{3,19},{4,68},{5,21},{6,70},{7,23},{8,72},{9,... | collective-permute-start | bytes 1572872 | tf_op jit(solution)/shard_map/ppermute | solution.py:56
  58.4 15.4 %collective-permute-start.17 = (f32[256,512]{1,0:T(8,128)S(1)}, f32[256,512]{1,0:T(8,128)S(1)}, u32[]{:S(2)}, u32[]{:S(2)}) collective-permute-start(f32[256,512]{1,0:T(8,128)S(1)} %broadcast_select_fusion.2), channel_id=1, source_target_pairs={{1,25},{3,27},{5,29},{7,31},{8,104},{9,17},{10,106},{11,19},{12,10... | collective-permute-start | bytes 1572872 | tf_op jit(solution)/shard_map/ppermute | solution.py:56
  64.0 42.2 %collective-permute-start.12 = (f32[2,512,512]{2,1,0:T(8,128)}, f32[2,512,512]{2,1,0:T(8,128)}, u32[]{:S(2)}, u32[]{:S(2)}) collective-permute-start(f32[2,512,512]{2,1,0:T(8,128)} %broadcast_select_fusion), channel_id=1, source_target_pairs={{0,6},{1,3},{2,4},{7,5},{8,14},{9,11},{10,12},{15,13},{16,22},{17,... | collective-permute-start | bytes 6291464 | tf_op jit(solution)/shard_map/ppermute | solution.py:56
  69.0 33.3 %copy-start.1 = (f32[2,512,512]{2,1,0:T(8,128)S(1)}, f32[2,512,512]{2,1,0:T(8,128)}, u32[]{:S(2)}) copy-start(f32[2,512,512]{2,1,0:T(8,128)} %inv_ref.1) | copy-start | bytes 6291460
  69.0 39.7 %collective-permute-start.10 = (f32[2,2048,128]{2,1,0:T(8,128)}, f32[2,2048,128]{2,1,0:T(8,128)}, u32[]{:S(2)}, u32[]{:S(2)}) collective-permute-start(f32[2,2048,128]{2,1,0:T(8,128)} %bitcast.28), channel_id=1, source_target_pairs={{0,24},{1,97},{2,26},{3,99},{4,28},{5,101},{6,30},{7,103},{8,0},{9... | collective-permute-start | bytes 6291464 | tf_op jit(solution)/shard_map/ppermute | solution.py:56
  69.0 39.7 %collective-permute-start.9 = (f32[2,2048,128]{2,1,0:T(8,128)}, f32[2,2048,128]{2,1,0:T(8,128)}, u32[]{:S(2)}, u32[]{:S(2)}) collective-permute-start(f32[2,2048,128]{2,1,0:T(8,128)} %bitcast.28), channel_id=1, source_target_pairs={{0,8},{1,33},{2,10},{3,35},{4,12},{5,37},{6,14},{7,39},{8,16},{9,4... | collective-permute-start | bytes 6291464 | tf_op jit(solution)/shard_map/ppermute | solution.py:56
  74.0 25.3 %collective-permute-start.18 = (f32[256,512]{1,0:T(8,128)S(1)}, f32[256,512]{1,0:T(8,128)S(1)}, u32[]{:S(2)}, u32[]{:S(2)}) collective-permute-start(f32[256,512]{1,0:T(8,128)S(1)} %select_select_fusion.2), channel_id=1, source_target_pairs={{1,33},{3,35},{5,37},{7,39},{8,16},{9,41},{10,18},{11,43},{12,20},... | collective-permute-start | bytes 1572872 | tf_op jit(solution)/shard_map/ppermute | solution.py:56
  100.1 16.2 %collective-permute-start.19 = (f32[256,512]{1,0:T(8,128)}, f32[256,512]{1,0:T(8,128)}, u32[]{:S(2)}, u32[]{:S(2)}) collective-permute-start(f32[256,512]{1,0:T(8,128)} %broadcast_select_fusion.3), channel_id=1, source_target_pairs={{1,97},{3,99},{5,101},{7,103},{8,0},{9,105},{10,2},{11,107},{12,4}... | collective-permute-start | bytes 1572872 | tf_op jit(solution)/shard_map/ppermute | solution.py:56
  108.7 18.0 %collective-permute-start.13 = (f32[2,512,512]{2,1,0:T(8,128)S(1)}, f32[2,512,512]{2,1,0:T(8,128)S(1)}, u32[]{:S(2)}, u32[]{:S(2)}) collective-permute-start(f32[2,512,512]{2,1,0:T(8,128)S(1)} %select_select_fusion.mine_ref), channel_id=1, source_target_pairs={{0,1},{1,0},{2,3},{3,2},{4,5},{5,4},{6,7},{7,6},{8,9},{9,8},{10,11... | collective-permute-start | bytes 6291464 | tf_op jit(solution)/shard_map/ppermute | solution.py:56
  117.5 3.3 %collective-permute-start.20 = (f32[256,512]{1,0:T(8,128)S(1)}, f32[256,512]{1,0:T(8,128)S(1)}, u32[]{:S(2)}, u32[]{:S(2)}) collective-permute-start(f32[256,512]{1,0:T(8,128)S(1)} %select_select_fusion.1), channel_id=1, source_target_pairs={{0,1},{1,0},{2,3},{3,2},{4,5},{5,4},{6,7},{7,6},{8,9},{9,8},{10,11... | collective-permute-start | bytes 1572872 | tf_op jit(solution)/shard_map/ppermute | solution.py:56
  122.3 25.7 %collective-permute-start.21 = (f32[2048,128]{1,0:T(8,128)S(1)}, f32[2048,128]{1,0:T(8,128)S(1)}, u32[]{:S(2)}, u32[]{:S(2)}) collective-permute-start(f32[2048,128]{1,0:T(8,128)S(1)} %slice_bitcast_fusion.1), channel_id=1, source_target_pairs={{0,8},{1,33},{2,10},{3,35},{4,12},{5,37},{6,14},{7,39},{8,16},{9,4... | collective-permute-start | bytes 3145736 | tf_op jit(solution)/shard_map/ppermute | solution.py:56
  124.8 23.2 %collective-permute-start.22 = (f32[2048,128]{1,0:T(8,128)S(1)}, f32[2048,128]{1,0:T(8,128)S(1)}, u32[]{:S(2)}, u32[]{:S(2)}) collective-permute-start(f32[2048,128]{1,0:T(8,128)S(1)} %slice_bitcast_fusion), channel_id=1, source_target_pairs={{0,24},{1,97},{2,26},{3,99},{4,28},{5,101},{6,30},{7,103},{8,0},{9... | collective-permute-start | bytes 3145736 | tf_op jit(solution)/shard_map/ppermute | solution.py:56
  (5 other events, 25.9 us)

commit v3 on v2

--- a/solution.py
+++ b/solution.py
@@ -11,7 +11,7 @@
 RING = 4
 MOVES = (1, -1, 2)
 SPLIT = 2
-VMEM_BYTES = 50 * 1024 * 1024
+VMEM_BYTES = 40 * 1024 * 1024
 
 
 def place(z, y, x, c):
@@ -186,16 +186,6 @@
     lanes = rhs.shape[2] // RING
     stride = RING * cbd
 
-    @pl.when((pl.program_id(0) == 0) & (pl.program_id(1) == 0))
-    def _():
-        for j in range(2 * count):
-            for c in range(cbd):
-                for t in range(RING):
-                    high, low = split(halves[j][pl.ds(t * cbd + c, half, stride=stride), :])
-                    for place_at, value in ((0, high), (1, low), (2, high)):
-                        start = (3 * (j // 2) + place_at) * depth + (j % 2) * half
-                        rhs[c, start : start + half, t * lanes : (t + 1) * lanes] = value
-
     left = []
     for kind in (1, 0):
         terms = []
@@ -203,11 +193,35 @@
             h, l = factors[4 * j + 2 * kind][0], factors[4 * j + 2 * kind + 1][0]
             terms += [h, h, l]
         left.append(jnp.concatenate(terms, axis=1))
-    for c in range(cbd):
+
+    def prepare(c):
+        for j in range(2 * count):
+            for t in range(RING):
+                high, low = split(halves[j][pl.ds(t * cbd + c, half, stride=stride), :])
+                for place_at, value in ((0, high), (1, low), (2, high)):
+                    start = (3 * (j // 2) + place_at) * depth + (j % 2) * half
+                    rhs[c, start : start + half, t * lanes : (t + 1) * lanes] = value
+
+    def subtract(c):
         product = dot(left[min(c, 1)], rhs[c])
         for t in range(RING):
             at = pl.ds(t * cbd + c, rows, stride=stride)
             out_ref[at, :] = x_ref[at, :] - product[:, t * lanes : (t + 1) * lanes]
+
+    first = (pl.program_id(0) == 0) & (pl.program_id(1) == 0)
+
+    @pl.when(first)
+    def _():
+        prepare(0)
+        for c in range(cbd):
+            if c + 1 < cbd:
+                prepare(c + 1)
+            subtract(c)
+
+    @pl.when(jnp.logical_not(first))
+    def _():
+        for c in range(cbd):
+            subtract(c)
 
 
 def subtract_products(lines, factors, ks, halves, cbd):
@@ -370,7 +384,6 @@
         return (z, y, 2, c) if x == sign(c) % RING else None
 
     s = jnp.where(c == 0, x, -x) % RING
-    start = share(start, s, pairs(x_first), pairs(x_second))
     mine = share(column, s, pairs(x_first), pairs(x_second))
     def uv(z, y, c):
         return (y, z) if c == 0 else (z, y)
@@ -380,26 +393,25 @@
 
     def v_first(z, y, x, c):
         u, v = uv(z, y, c)
-        return zyxc(u, 1, x, c) if v == 0 and u == 1 - c else None
+        return zyxc(u, 1, x, c) if x == 0 and v == 0 and u == 1 - c else None
 
     def v_second(z, y, x, c):
         u, v = uv(z, y, c)
-        return zyxc(u, 3 if v == 0 else 2, x, c) if v < 2 and u == 1 - c else None
+        return zyxc(u, 3 if v == 0 else 2, x, c) if x == 0 and v < 2 and u == 1 - c else None
 
     def u_first(z, y, x, c):
         u, v = uv(z, y, c)
-        return zyxc(u + 1, v, x, c) if u == 1 - c else None
+        return zyxc(u + 1, v, x, c) if x == 0 and u == 1 - c else None
 
     def u_second(z, y, x, c):
         u, v = uv(z, y, c)
         w = (u - 1 + c) % RING
-        return zyxc(u - 1 if w == 0 else u + 1, v, x, c) if w < 2 else None
+        return zyxc(u - 1 if w == 0 else u + 1, v, x, c) if x == 0 and w < 2 else None
 
     line = share(start, v, pairs(v_first), pairs(v_second))
-    here = share(line, (u - 1 + c) % RING, pairs(u_first), pairs(u_second))
-    there = other_core(here)
-    corner = jnp.concatenate([jnp.where(c == 0, here, there), jnp.where(c == 0, there, here)])
-    return mine, corner
+    plane = share(line, (u - 1 + c) % RING, pairs(u_first), pairs(u_second))
+    here = share(plane, s, pairs(x_first), pairs(x_second))
+    return mine, here
 
 
 def body(matrix, inverse_factors):
@@ -414,12 +426,15 @@
     lines = to_lines(matrix)
     own, before, after = top_rows(lines, u, v, c)
     start = corner_half(c.astype(jnp.int32)[None], lines, nb, cbd)
-    mine, corner = row_inputs(first_column(lines, rbd, nb, cbd), start, u, v, x, c)
+    mine, here = row_inputs(first_column(lines, rbd, nb, cbd), start, u, v, x, c)
     before, after, mine, turned = lax.optimization_barrier(
         (before, after, mine, weights(inverse_factors))
     )
     far = send(before[0], along_u(1)), send(after[1], along_u(-1))
-    theirs = other_core(mine)
+    both = jnp.concatenate([mine.reshape(-1, nb), here])
+    swapped = other_core(both)
+    theirs, there = swapped[: rbd * nb].reshape(mine.shape), swapped[rbd * nb :]
+    corner = jnp.concatenate([jnp.where(c == 0, here, there), jnp.where(c == 0, there, here)])
 
     where = jnp.stack([prow, pcol, c]).astype(jnp.int32)
     panels, *factors = row_factors(where, mine, theirs, corner, *turned)

time: 179 us -> 166 us (0.927); the launches traced: 176 us -> 166 us
  Pallas kernels: 58.3 us -> 50.9 us
  waiting for transfers between devices: 49.6 us -> 44.9 us
  starting transfers between devices: 35.6 us -> 38.1 us
    ppermute x23 -> x22, waiting for transfers between devices: 49.6 us -> 44.9 us  [send(): return lax.ppermute(x, AXES, moves)]
    pallas_call x1, Pallas kernels: 27.6 us -> 25.1 us  [subtract_products(): pl.pallas_call(functools.partial(update_kernel, count), grid_spec=pltpu.P...]
    dynamic_update_slice x3, local copies, waits for them, and re-layouts: 2.6 us -> 0.12 us  [ring_order(): whole = lax.dynamic_update_slice(whole, value[:, None], start)]
    ppermute x23 -> x22, starting transfers between devices: 35.6 us -> 38.1 us  [send(): return lax.ppermute(x, AXES, moves)]
    unnamed x12, local copies, waits for them, and re-layouts: 2.73 us -> 4.99 us
    pallas_call x1, Pallas kernels: 2.51 us -> 0.32 us  [corner_half(): pl.pallas_call(corner_kernel, grid=(1,), in_specs=[pl.BlockSpec(memory_sp...]
    pallas_call x1, Pallas kernels: 4.04 us -> 1.97 us  [weights(): pl.pallas_call(weights_kernel, out_shape=[jax.ShapeDtypeStruct((3 * nb, 2...]
  transfers between devices with their start and end apart: 23 -> 22, of which waited for: 7 -> 4; matrix products, arithmetic and copies ran while one was open for 14% -> 13% of each run, Pallas kernels for 17% -> 16%
where the time goes in v3:
time: 166 us
  Pallas kernels  50.9 us (31%)
  waiting for transfers between devices  44.9 us (27%)
  starting transfers between devices  38.1 us (23%)
  other arithmetic  18 us (11%)
  local copies, waits for them, and re-layouts  12.6 us (8%)
    ppermute x22, waiting for transfers between devices, send(): return lax.ppermute(x, AXES, moves)  44.9 us
    ppermute x22, starting transfers between devices, send(): return lax.ppermute(x, AXES, moves)  38.1 us
    pallas_call x1, Pallas kernels, subtract_products(): pl.pallas_call(functools.partial(update_kernel, count), grid_spec=pltpu.P...  25.1 us
    pallas_call x1, Pallas kernels, row_factors(): pl.pallas_call(factors_kernel, grid=(rbd, SPLIT), in_specs=[pl.BlockSpec(...  18 us
    pallas_call x1, Pallas kernels, first_column(): pl.pallas_call(column_kernel, grid=(rbd, 2), in_specs=[pl.BlockSpec((tile...  5.56 us
    select_n x4, other arithmetic, share(): two = send(jnp.where(index == 0, x, one), second)  5.32 us
    unnamed x12, local copies, waits for them, and re-layouts  4.99 us
    select_n x4, other arithmetic, choose(): result = jnp.where(index == i, options[i], result)  4.88 us
  transfers between devices with their start and end apart: 22, of which 4 were waited for; matrix products, arithmetic and copies ran while one was open for 13% of the time, Pallas kernels for 16%

profile of v3, /device:TPU:21, one launch (start us, length us, event | category | flops | bytes accessed | tf_op | source)
XLA Modules:
  0.0 165.5 jit_solution(2945662963321273752)
XLA Ops:
  0.7 3.6 %constant_dynamic-slice_fusion.2 = (f32[2048,128]{1,0:T(8,128)}, f32[2048,128]{1,0:T(8,128)}, f32[2048,128]{1,0:T(8,128)}) fusion(f32[16384,128]{1,0:T(8,128)} %bitcast.85, s32[]{:T(128)S(6)} %select_n.400, s32[]{:T(128)S(6)} %select_n.405, s32[]{:T(128)S(6)} %select_n.403), kind=kLoop, calls=%fused_computation.41 | loop fusion | bytes 6291468 | tf_op jit(solution)/shard_map/dynamic_slice | solution.py:340
  5.8 1.6 collective-permute-start.2
  7.5 3.4 %copy-done = f32[2,512,4,512]{3,2,1,0:T(4,128)S(1)} copy-done((f32[2,512,4,512]{3,2,1,0:T(4,128)S(1)}, f32[2,512,4,512]{3,2,1,0:T(4,128)}, u32[]{:S(2)}) %copy-start) | copy-done | bytes 8388632
  11.9 5.6 %shard_map.41 = f32[2,512,512]{2,1,0:T(8,128)} custom-call(f32[16384,128]{1,0:T(8,128)} %bitcast.86), custom_call_target="tpu_custom_call" | custom-call | bytes 10485760 | tf_op jit(solution)/shard_map/pallas_call | solution.py:274
  17.4 2.0 %collective-permute-start.11 = (f32[2,512,512]{2,1,0:T(8,128)}, f32[2,512,512]{2,1,0:T(8,128)}, u32[]{:S(2)}, u32[]{:S(2)}) collective-permute-start(f32[2,512,512]{2,1,0:T(8,128)} %shard_map.41), channel_id=1, source_target_pairs={{0,2},{1,7},{8,10},{9,15},{16,18},{17,23},{24,26},{25,31},{32,34},... | collective-permute-start | bytes 6291464 | tf_op jit(solution)/shard_map/ppermute | solution.py:56
  20.3 1.5 collective-permute-start.14
  21.8 1.6 select_bitcast_fusion.6
  28.5 1.5 collective-permute-start.5
  31.8 10.7 %collective-permute-done.3 = f32[2,512,128]{2,1,0:T(8,128)} collective-permute-done((f32[2,512,128]{2,1,0:T(8,128)}, f32[2,512,128]{2,1,0:T(8,128)}, u32[]{:S(2)}, u32[]{:S(2)}) %collective-permute-start.3) | collective-permute-done | bytes 524320 | tf_op jit(solution)/shard_map/ppermute | solution.py:56
  42.5 6.8 %collective-permute-done.4 = f32[2,512,128]{2,1,0:T(8,128)} collective-permute-done((f32[2,512,128]{2,1,0:T(8,128)}, f32[2,512,128]{2,1,0:T(8,128)}, u32[]{:S(2)}, u32[]{:S(2)}) %collective-permute-start.4) | collective-permute-done | bytes 524320 | tf_op jit(solution)/shard_map/ppermute | solution.py:56
  50.7 1.6 fusion.4
  52.4 2.8 %collective-permute-start.6 = (f32[2,512,128]{2,1,0:T(8,128)S(1)}, f32[2,512,128]{2,1,0:T(8,128)S(1)}, u32[]{:S(2)}, u32[]{:S(2)}) collective-permute-start(f32[2,512,128]{2,1,0:T(8,128)S(1)} %pad_maximum_fusion.5), channel_id=1, source_target_pairs={{0,32},{1,9},{2,34},{3,11},{4,36},{5,13},{6,38},{7,15},{8,40},{9,1... | collective-permute-start | bytes 1572872 | tf_op jit(solution)/shard_map/ppermute | solution.py:56
  55.2 2.2 %collective-permute-start.8 = (f32[2,512,128]{2,1,0:T(8,128)S(1)}, f32[2,512,128]{2,1,0:T(8,128)S(1)}, u32[]{:S(2)}, u32[]{:S(2)}) collective-permute-start(f32[2,512,128]{2,1,0:T(8,128)S(1)} %pad_maximum_fusion.5), channel_id=1, source_target_pairs={{0,64},{1,17},{2,66},{3,19},{4,68},{5,21},{6,70},{7,23},{8,72},{9,... | collective-permute-start | bytes 1572872 | tf_op jit(solution)/shard_map/ppermute | solution.py:56
  58.5 3.5 %broadcast_select_fusion = f32[2,512,512]{2,1,0:T(8,128)} fusion(f32[2,512,512]{2,1,0:T(8,128)S(1)} %copy-done.4, f32[2,512,512]{2,1,0:T(8,128)} %collective-permute-done.11, pred[]{:T(512)S(6)} %eq.47), kind=kLoop, calls=%fused_computation.5 | loop fusion | flops 524288 | bytes 6291457 | tf_op jit(solution)/shard_map/jit(_where)/select_n | solution.py:331
  63.4 3.9 %collective-permute-done.8 = f32[2,512,128]{2,1,0:T(8,128)S(1)} collective-permute-done((f32[2,512,128]{2,1,0:T(8,128)S(1)}, f32[2,512,128]{2,1,0:T(8,128)S(1)}, u32[]{:S(2)}, u32[]{:S(2)}) %collective-permute-start.8) | collective-permute-done | bytes 524320 | tf_op jit(solution)/shard_map/ppermute | solution.py:56
  71.9 1.6 copy-done.1
  73.5 2.0 %shard_map.42 = (bf16[1536,1024]{1,0:T(8,128)(2,1)S(1)}, bf16[1536,1024]{1,0:T(8,128)(2,1)S(1)}) custom-call(f32[2,512,512]{2,1,0:T(8,128)S(1)} %copy-done.1), custom_call_target="tpu_custom_call" | custom-call | flops 2000000000 | bytes 8388608 | tf_op jit(solution)/shard_map/pallas_call | solution.py:113
  75.5 23.4 %collective-permute-done.18 = f32[256,512]{1,0:T(8,128)} collective-permute-done((f32[256,512]{1,0:T(8,128)}, f32[256,512]{1,0:T(8,128)}, u32[]{:S(2)}, u32[]{:S(2)}) %collective-permute-start.18) | collective-permute-done | bytes 524320 | tf_op jit(solution)/shard_map/ppermute | solution.py:56
  100.1 2.4 %select_select_fusion.mine_ref = f32[2,512,512]{2,1,0:T(8,128)S(1)} fusion(f32[2,512,512]{2,1,0:T(8,128)S(1)} %copy-done.5, f32[2,512,512]{2,1,0:T(8,128)} %collective-permute-done.11, f32[2,512,512]{2,1,0:T(8,128)} %collective-permute-done.12, pred[]{:T(512)S(6)} %eq.48, pred[]{:T(512)S(6)} %eq.47), kind=kLoop, calls=%fused_computation.1 | loop fusion | flops 1048576 | bytes 8388610 | tf_op jit(solution)/shard_map/jit(_where)/select_n | solution.py:66
  102.8 12.9 %collective-permute-start.19 = (f32[1280,512]{1,0:T(8,128)S(1)}, f32[1280,512]{1,0:T(8,128)S(1)}, u32[]{:S(2)}, u32[]{:S(2)}) collective-permute-start(f32[1280,512]{1,0:T(8,128)S(1)} %pad_maximum_fusion), channel_id=1, source_target_pairs={{0,1},{1,0},{2,3},{3,2},{4,5},{5,4},{6,7},{7,6},{8,9},{9,8},{10,11... | collective-permute-start | bytes 7864328 | tf_op jit(solution)/shard_map/ppermute | solution.py:56
  117.3 2.3 %slice_bitcast_fusion = f32[2048,128]{1,0:T(8,128)} fusion(f32[2,2048,128]{2,1,0:T(8,128)} %collective-permute-done.10), kind=kLoop, calls=%fused_computation.3 | loop fusion | bytes 2097152 | tf_op jit(solution)/shard_map/squeeze | solution.py:433
  119.6 2.5 %collective-permute-start.21 = (f32[2048,128]{1,0:T(8,128)}, f32[2048,128]{1,0:T(8,128)S(1)}, u32[]{:S(2)}, u32[]{:S(2)}) collective-permute-start(f32[2048,128]{1,0:T(8,128)} %slice_bitcast_fusion), channel_id=1, source_target_pairs={{0,24},{1,97},{2,26},{3,99},{4,28},{5,101},{6,30},{7,103},{8,0},{9... | collective-permute-start | bytes 3145736 | tf_op jit(solution)/shard_map/ppermute | solution.py:56
  122.5 18.0 %shard_map.44 = (f32[2,2,512,512]{3,2,1,0:T(8,128)}, bf16[4,1024,256]{2,1,0:T(8,128)(2,1)S(1)}, bf16[4,1024,256]{2,1,0:T(8,128)(2,1)S(1)}, bf16[4,1024,256]{2,1,0:T(8,128)(2,1)S(1)}, bf16[4,1024,256]{2,1,0:T(8,128)(2,1)S(1)}) custom-call(s32[3]{0:T(128)S(1)} %pad_add_fusion.where_ref, f32[2,512,512]{2,1,0:T(8,128)S(1)} %select_select_fusion.mine_ref, ...), custom_call_target="tpu_custom_call" | custom-call | flops 11000000512 | bytes 25165824 | tf_op jit(solution)/shard_map/pallas_call | solution.py:168
  140.5 25.1 %shard_map.45 = f32[16384,128]{1,0:T(8,128)} custom-call(s32[4]{0:T(128)S(1)} %and_select_fusion.ks_ref, f32[16384,128]{1,0:T(8,128)} %bitcast.90, bf16[4,1024,256]{2,1,0:T(8,128)(2,1)S(1)} %get-tuple-element.32.rest_0_.rest_4_.rest_8_.rest_12_, bf16[4,1024,256]{2,1,0:T(8,128)(2,1)S(1)} %get-tuple-element.33.rest_1_.rest_5_.rest_9_.rest_13_, ...), custom_call_target="tpu_custom_call" | custom-call | flops 13200000000 | bytes 33554432 | tf_op jit(solution)/shard_map/pallas_call | solution.py:246
  (66 shorter events, 22.1 us)
Async XLA Ops:
  4.3 17.4 %collective-permute-start = (f32[2048,128]{1,0:T(8,128)}, f32[2048,128]{1,0:T(8,128)S(1)}, u32[]{:S(2)}, u32[]{:S(2)}) collective-permute-start(f32[2048,128]{1,0:T(8,128)} %get-tuple-element.44), channel_id=1, source_target_pairs={{0,8},{1,33},{2,10},{3,35},{4,12},{5,37},{6,14},{7,39},{8,16},{9,4... | collective-permute-start | bytes 3145736 | tf_op jit(solution)/shard_map/ppermute | solution.py:56
  5.1 16.7 %collective-permute-start.1 = (f32[2048,128]{1,0:T(8,128)}, f32[2048,128]{1,0:T(8,128)S(1)}, u32[]{:S(2)}, u32[]{:S(2)}) collective-permute-start(f32[2048,128]{1,0:T(8,128)} %get-tuple-element.46), channel_id=1, source_target_pairs={{0,16},{1,65},{2,18},{3,67},{4,20},{5,69},{6,22},{7,71},{8,24},{9,... | collective-permute-start | bytes 3145736 | tf_op jit(solution)/shard_map/ppermute | solution.py:56
  5.8 16.0 %collective-permute-start.2 = (f32[2048,128]{1,0:T(8,128)}, f32[2048,128]{1,0:T(8,128)}, u32[]{:S(2)}, u32[]{:S(2)}) collective-permute-start(f32[2048,128]{1,0:T(8,128)} %get-tuple-element.45), channel_id=1, source_target_pairs={{0,24},{1,97},{2,26},{3,99},{4,28},{5,101},{6,30},{7,103},{8,0},{9... | collective-permute-start | bytes 3145736 | tf_op jit(solution)/shard_map/ppermute | solution.py:56
  11.2 8.3 %collective-permute-start.13 = (f32[256,512]{1,0:T(8,128)S(1)}, f32[256,512]{1,0:T(8,128)S(1)}, u32[]{:S(2)}, u32[]{:S(2)}) collective-permute-start(f32[256,512]{1,0:T(8,128)S(1)} %shard_map.43), channel_id=1, source_target_pairs={{1,9},{8,40}} | collective-permute-start | bytes 1572872 | tf_op jit(solution)/shard_map/ppermute | solution.py:56
  17.4 41.0 %collective-permute-start.11 = (f32[2,512,512]{2,1,0:T(8,128)}, f32[2,512,512]{2,1,0:T(8,128)}, u32[]{:S(2)}, u32[]{:S(2)}) collective-permute-start(f32[2,512,512]{2,1,0:T(8,128)} %shard_map.41), channel_id=1, source_target_pairs={{0,2},{1,7},{8,10},{9,15},{16,18},{17,23},{24,26},{25,31},{32,34},... | collective-permute-start | bytes 6291464 | tf_op jit(solution)/shard_map/ppermute | solution.py:56
  20.3 9.6 %collective-permute-start.14 = (f32[256,512]{1,0:T(8,128)}, f32[256,512]{1,0:T(8,128)}, u32[]{:S(2)}, u32[]{:S(2)}) collective-permute-start(f32[256,512]{1,0:T(8,128)} %broadcast_select_fusion.1), channel_id=1, source_target_pairs={{1,25},{8,104},{9,17},{40,72}} | collective-permute-start | bytes 1572872 | tf_op jit(solution)/shard_map/ppermute | solution.py:56
  24.2 18.3 %collective-permute-start.3 = (f32[2,512,128]{2,1,0:T(8,128)}, f32[2,512,128]{2,1,0:T(8,128)}, u32[]{:S(2)}, u32[]{:S(2)}) collective-permute-start(f32[2,512,128]{2,1,0:T(8,128)} %pad_maximum_fusion.2), channel_id=1, source_target_pairs={{0,32},{1,9},{2,34},{3,11},{4,36},{5,13},{6,38},{7,15},{8,40},{9,1... | collective-permute-start | bytes 1572872 | tf_op jit(solution)/shard_map/ppermute | solution.py:56
  26.3 23.0 %collective-permute-start.4 = (f32[2,512,128]{2,1,0:T(8,128)}, f32[2,512,128]{2,1,0:T(8,128)}, u32[]{:S(2)}, u32[]{:S(2)}) collective-permute-start(f32[2,512,128]{2,1,0:T(8,128)} %pad_maximum_fusion.3), channel_id=1, source_target_pairs={{0,64},{1,17},{2,66},{3,19},{4,68},{5,21},{6,70},{7,23},{8,72},{9,... | collective-permute-start | bytes 1572872 | tf_op jit(solution)/shard_map/ppermute | solution.py:56
  28.5 20.8 %collective-permute-start.5 = (f32[2,512,128]{2,1,0:T(8,128)}, f32[2,512,128]{2,1,0:T(8,128)}, u32[]{:S(2)}, u32[]{:S(2)}) collective-permute-start(f32[2,512,128]{2,1,0:T(8,128)} %pad_maximum_fusion.4), channel_id=1, source_target_pairs={{0,96},{1,25},{2,98},{3,27},{4,100},{5,29},{6,102},{7,31},{8,104},... | collective-permute-start | bytes 1572872 | tf_op jit(solution)/shard_map/ppermute | solution.py:56
  31.1 26.3 %collective-permute-start.15 = (f32[256,512]{1,0:T(8,128)S(1)}, f32[256,512]{1,0:T(8,128)S(1)}, u32[]{:S(2)}, u32[]{:S(2)}) collective-permute-start(f32[256,512]{1,0:T(8,128)S(1)} %select_select_fusion.3), channel_id=1, source_target_pairs={{1,33},{8,16},{9,41},{17,49},{25,57},{40,48},{72,80},{104,112}} | collective-permute-start | bytes 1572872 | tf_op jit(solution)/shard_map/ppermute | solution.py:56
  52.4 10.8 %collective-permute-start.6 = (f32[2,512,128]{2,1,0:T(8,128)S(1)}, f32[2,512,128]{2,1,0:T(8,128)S(1)}, u32[]{:S(2)}, u32[]{:S(2)}) collective-permute-start(f32[2,512,128]{2,1,0:T(8,128)S(1)} %pad_maximum_fusion.5), channel_id=1, source_target_pairs={{0,32},{1,9},{2,34},{3,11},{4,36},{5,13},{6,38},{7,15},{8,40},{9,1... | collective-permute-start | bytes 1572872 | tf_op jit(solution)/shard_map/ppermute | solution.py:56
  55.2 8.1 %collective-permute-start.7 = (f32[2,512,128]{2,1,0:T(8,128)S(1)}, f32[2,512,128]{2,1,0:T(8,128)S(1)}, u32[]{:S(2)}, u32[]{:S(2)}) collective-permute-start(f32[2,512,128]{2,1,0:T(8,128)S(1)} %pad_maximum_fusion.5), channel_id=1, source_target_pairs={{0,96},{1,25},{2,98},{3,27},{4,100},{5,29},{6,102},{7,31},{8,104},... | collective-permute-start | bytes 1572872 | tf_op jit(solution)/shard_map/ppermute | solution.py:56
  55.2 12.1 %collective-permute-start.8 = (f32[2,512,128]{2,1,0:T(8,128)S(1)}, f32[2,512,128]{2,1,0:T(8,128)S(1)}, u32[]{:S(2)}, u32[]{:S(2)}) collective-permute-start(f32[2,512,128]{2,1,0:T(8,128)S(1)} %pad_maximum_fusion.5), channel_id=1, source_target_pairs={{0,64},{1,17},{2,66},{3,19},{4,68},{5,21},{6,70},{7,23},{8,72},{9,... | collective-permute-start | bytes 1572872 | tf_op jit(solution)/shard_map/ppermute | solution.py:56
  57.5 11.3 %collective-permute-start.16 = (f32[256,512]{1,0:T(8,128)S(1)}, f32[256,512]{1,0:T(8,128)S(1)}, u32[]{:S(2)}, u32[]{:S(2)}) collective-permute-start(f32[256,512]{1,0:T(8,128)S(1)} %broadcast_select_fusion.2), channel_id=1, source_target_pairs={{1,97},{8,0},{9,105},{16,24},{17,113},{25,121},{33,65},{40,32},{41... | collective-permute-start | bytes 1572872 | tf_op jit(solution)/shard_map/ppermute | solution.py:56
  61.9 38.2 %collective-permute-start.12 = (f32[2,512,512]{2,1,0:T(8,128)}, f32[2,512,512]{2,1,0:T(8,128)}, u32[]{:S(2)}, u32[]{:S(2)}) collective-permute-start(f32[2,512,512]{2,1,0:T(8,128)} %broadcast_select_fusion), channel_id=1, source_target_pairs={{0,6},{1,3},{2,4},{7,5},{8,14},{9,11},{10,12},{15,13},{16,22},{17,... | collective-permute-start | bytes 6291464 | tf_op jit(solution)/shard_map/ppermute | solution.py:56
  67.3 35.2 %collective-permute-start.10 = (f32[2,2048,128]{2,1,0:T(8,128)S(1)}, f32[2,2048,128]{2,1,0:T(8,128)}, u32[]{:S(2)}, u32[]{:S(2)}) collective-permute-start(f32[2,2048,128]{2,1,0:T(8,128)S(1)} %bitcast.92), channel_id=1, source_target_pairs={{0,24},{1,97},{2,26},{3,99},{4,28},{5,101},{6,30},{7,103},{8,0},{9... | collective-permute-start | bytes 6291464 | tf_op jit(solution)/shard_map/ppermute | solution.py:56
  67.4 35.1 %collective-permute-start.9 = (f32[2,2048,128]{2,1,0:T(8,128)S(1)}, f32[2,2048,128]{2,1,0:T(8,128)}, u32[]{:S(2)}, u32[]{:S(2)}) collective-permute-start(f32[2,2048,128]{2,1,0:T(8,128)S(1)} %bitcast.93), channel_id=1, source_target_pairs={{0,8},{1,33},{2,10},{3,35},{4,12},{5,37},{6,14},{7,39},{8,16},{9,4... | collective-permute-start | bytes 6291464 | tf_op jit(solution)/shard_map/ppermute | solution.py:56
  69.0 0.7 collective-permute-start.17
  70.6 28.3 %collective-permute-start.18 = (f32[256,512]{1,0:T(8,128)}, f32[256,512]{1,0:T(8,128)}, u32[]{:S(2)}, u32[]{:S(2)}) collective-permute-start(f32[256,512]{1,0:T(8,128)} %broadcast_select_fusion.3), channel_id=1, source_target_pairs={{0,6},{1,3},{2,4},{7,5},{8,14},{9,11},{10,12},{15,13},{16,22},{17,... | collective-permute-start | bytes 1572872 | tf_op jit(solution)/shard_map/ppermute | solution.py:56
  75.4 27.1 %copy-start.2 = (bf16[1536,1024]{1,0:T(8,128)(2,1)}, bf16[1536,1024]{1,0:T(8,128)(2,1)S(1)}, u32[]{:S(2)}) copy-start(bf16[1536,1024]{1,0:T(8,128)(2,1)S(1)} %get-tuple-element.23.first_ref) | copy-start | bytes 9437188
  75.5 27.1 %copy-start.3 = (bf16[1536,1024]{1,0:T(8,128)(2,1)}, bf16[1536,1024]{1,0:T(8,128)(2,1)S(1)}, u32[]{:S(2)}) copy-start(bf16[1536,1024]{1,0:T(8,128)(2,1)S(1)} %get-tuple-element.24.second_ref) | copy-start | bytes 9437188
  102.8 19.3 %collective-permute-start.19 = (f32[1280,512]{1,0:T(8,128)S(1)}, f32[1280,512]{1,0:T(8,128)S(1)}, u32[]{:S(2)}, u32[]{:S(2)}) collective-permute-start(f32[1280,512]{1,0:T(8,128)S(1)} %pad_maximum_fusion), channel_id=1, source_target_pairs={{0,1},{1,0},{2,3},{3,2},{4,5},{5,4},{6,7},{7,6},{8,9},{9,8},{10,11... | collective-permute-start | bytes 7864328 | tf_op jit(solution)/shard_map/ppermute | solution.py:56
  117.1 23.4 %collective-permute-start.20 = (f32[2048,128]{1,0:T(8,128)S(1)}, f32[2048,128]{1,0:T(8,128)S(1)}, u32[]{:S(2)}, u32[]{:S(2)}) collective-permute-start(f32[2048,128]{1,0:T(8,128)S(1)} %slice_bitcast_fusion.1), channel_id=1, source_target_pairs={{0,8},{1,33},{2,10},{3,35},{4,12},{5,37},{6,14},{7,39},{8,16},{9,4... | collective-permute-start | bytes 3145736 | tf_op jit(solution)/shard_map/ppermute | solution.py:56
  119.6 20.9 %collective-permute-start.21 = (f32[2048,128]{1,0:T(8,128)}, f32[2048,128]{1,0:T(8,128)S(1)}, u32[]{:S(2)}, u32[]{:S(2)}) collective-permute-start(f32[2048,128]{1,0:T(8,128)} %slice_bitcast_fusion), channel_id=1, source_target_pairs={{0,24},{1,97},{2,26},{3,99},{4,28},{5,101},{6,30},{7,103},{8,0},{9... | collective-permute-start | bytes 3145736 | tf_op jit(solution)/shard_map/ppermute | solution.py:56
  (4 other events, 35.7 us)

commit v4 on v3

--- a/solution.py
+++ b/solution.py
@@ -11,7 +11,8 @@
 RING = 4
 MOVES = (1, -1, 2)
 SPLIT = 2
-VMEM_BYTES = 40 * 1024 * 1024
+VMEM_BYTES = 36 * 1024 * 1024
+SMALL_VMEM_BYTES = 24 * 1024 * 1024
 
 
 def place(z, y, x, c):
@@ -114,7 +115,7 @@
         weights_kernel,
         out_shape=[jax.ShapeDtypeStruct((3 * nb, 2 * nb), jnp.bfloat16)] * 2,
         scratch_shapes=[pltpu.VMEM((3 * nb, nb), jnp.bfloat16)],
-        compiler_params=pltpu.CompilerParams(vmem_limit_bytes=VMEM_BYTES),
+        compiler_params=pltpu.CompilerParams(vmem_limit_bytes=SMALL_VMEM_BYTES),
         cost_estimate=pl.CostEstimate(flops=2 * 10**9, bytes_accessed=8 * 2**20, transcendentals=0),
     )(inverse_factors)
 
@@ -172,7 +173,7 @@
         out_specs=[pl.BlockSpec((2, 1, tile, nb), lambda a, t: (0, a, t, 0))] + [parts] * 4,
         out_shape=[jax.ShapeDtypeStruct((2, rbd, nb, nb), jnp.float32)] + [parts_shape] * 4,
         scratch_shapes=[pltpu.VMEM((3 * nb, nb), jnp.bfloat16)] * 2,
-        compiler_params=pltpu.CompilerParams(vmem_limit_bytes=VMEM_BYTES),
+        compiler_params=pltpu.CompilerParams(vmem_limit_bytes=SMALL_VMEM_BYTES),
         cost_estimate=pl.CostEstimate(flops=11 * 10**9, bytes_accessed=24 * 2**20, transcendentals=0),
     )(where, mine, theirs, corner, first, second)
 
@@ -309,7 +310,7 @@
         ],
         out_specs=pl.BlockSpec((nb // 2, nb), lambda i: (0, 0)),
         out_shape=jax.ShapeDtypeStruct((nb // 2, nb), lines.dtype),
-        compiler_params=pltpu.CompilerParams(vmem_limit_bytes=VMEM_BYTES),
+        compiler_params=pltpu.CompilerParams(vmem_limit_bytes=SMALL_VMEM_BYTES),
         cost_estimate=pl.CostEstimate(flops=0, bytes_accessed=5 * 2**20, transcendentals=0),
     )(core, lines)
 

time: 166 us -> 163 us (0.982)
  Pallas kernels: 50.9 us -> 48.6 us
    pallas_call x1, Pallas kernels: 18 us -> 15.7 us  [row_factors(): pl.pallas_call(factors_kernel, grid=(rbd, SPLIT), in_specs=[pl.BlockSpec(...]
    unnamed x12 -> x8, local copies, waits for them, and re-layouts: 4.99 us -> 4.98 us
  transfers between devices with their start and end apart: 22 -> 22, of which waited for: 4 -> 5; matrix products, arithmetic and copies ran while one was open for 13% -> 13% of each run, Pallas kernels for 16% -> 14%
where the time goes in v4:
time: 163 us
  Pallas kernels  48.6 us (30%)
  waiting for transfers between devices  45 us (28%)
  starting transfers between devices  38.4 us (24%)
  other arithmetic  18 us (11%)
  local copies, waits for them, and re-layouts  11.6 us (7%)
    ppermute x22, waiting for transfers between devices, send(): return lax.ppermute(x, AXES, moves)  45 us
    ppermute x22, starting transfers between devices, send(): return lax.ppermute(x, AXES, moves)  38.4 us
    pallas_call x1, Pallas kernels, subtract_products(): pl.pallas_call(functools.partial(update_kernel, count), grid_spec=pltpu.P...  25 us
    pallas_call x1, Pallas kernels, row_factors(): pl.pallas_call(factors_kernel, grid=(rbd, SPLIT), in_specs=[pl.BlockSpec(...  15.7 us
    pallas_call x1, Pallas kernels, first_column(): pl.pallas_call(column_kernel, grid=(rbd, 2), in_specs=[pl.BlockSpec((tile...  5.56 us
    select_n x4, other arithmetic, share(): two = send(jnp.where(index == 0, x, one), second)  5.32 us
    unnamed x8, local copies, waits for them, and re-layouts  4.98 us
    select_n x4, other arithmetic, choose(): result = jnp.where(index == i, options[i], result)  4.88 us
  transfers between devices with their start and end apart: 22, of which 5 were waited for; matrix products, arithmetic and copies ran while one was open for 13% of the time, Pallas kernels for 14%

profile of v4, /device:TPU:21, one launch (start us, length us, event | category | flops | bytes accessed | tf_op | source)
XLA Modules:
  0.0 162.7 jit_solution(17554012722461285635)
XLA Ops:
  0.7 3.6 %constant_dynamic-slice_fusion.2 = (f32[2048,128]{1,0:T(8,128)}, f32[2048,128]{1,0:T(8,128)}, f32[2048,128]{1,0:T(8,128)}) fusion(f32[16384,128]{1,0:T(8,128)} %bitcast.85, s32[]{:T(128)S(6)} %select_n.400, s32[]{:T(128)S(6)} %select_n.405, s32[]{:T(128)S(6)} %select_n.403), kind=kLoop, calls=%fused_computation.41 | loop fusion | bytes 6291468 | tf_op jit(solution)/shard_map/dynamic_slice | solution.py:341
  5.8 1.6 %collective-permute-start.2 = (f32[2048,128]{1,0:T(8,128)}, f32[2048,128]{1,0:T(8,128)}, u32[]{:S(2)}, u32[]{:S(2)}) collective-permute-start(f32[2048,128]{1,0:T(8,128)} %get-tuple-element.45), channel_id=1, source_target_pairs={{0,24},{1,97},{2,26},{3,99},{4,28},{5,101},{6,30},{7,103},{8,0},{9... | collective-permute-start | bytes 3145736 | tf_op jit(solution)/shard_map/ppermute | solution.py:57
  7.5 3.4 %copy-done = f32[2,512,4,512]{3,2,1,0:T(4,128)S(1)} copy-done((f32[2,512,4,512]{3,2,1,0:T(4,128)S(1)}, f32[2,512,4,512]{3,2,1,0:T(4,128)}, u32[]{:S(2)}) %copy-start) | copy-done | bytes 8388632
  11.9 5.6 %shard_map.41 = f32[2,512,512]{2,1,0:T(8,128)} custom-call(f32[16384,128]{1,0:T(8,128)} %bitcast.86), custom_call_target="tpu_custom_call" | custom-call | bytes 10485760 | tf_op jit(solution)/shard_map/pallas_call | solution.py:275
  17.4 2.0 %collective-permute-start.11 = (f32[2,512,512]{2,1,0:T(8,128)}, f32[2,512,512]{2,1,0:T(8,128)}, u32[]{:S(2)}, u32[]{:S(2)}) collective-permute-start(f32[2,512,512]{2,1,0:T(8,128)} %shard_map.41), channel_id=1, source_target_pairs={{0,2},{1,7},{8,10},{9,15},{16,18},{17,23},{24,26},{25,31},{32,34},... | collective-permute-start | bytes 6291464 | tf_op jit(solution)/shard_map/ppermute | solution.py:57
  20.3 1.5 collective-permute-start.14
  21.8 1.6 select_bitcast_fusion.6
  28.5 1.5 collective-permute-start.5
  31.9 10.7 %collective-permute-done.3 = f32[2,512,128]{2,1,0:T(8,128)} collective-permute-done((f32[2,512,128]{2,1,0:T(8,128)}, f32[2,512,128]{2,1,0:T(8,128)}, u32[]{:S(2)}, u32[]{:S(2)}) %collective-permute-start.3) | collective-permute-done | bytes 524320 | tf_op jit(solution)/shard_map/ppermute | solution.py:57
  42.6 6.8 %collective-permute-done.4 = f32[2,512,128]{2,1,0:T(8,128)} collective-permute-done((f32[2,512,128]{2,1,0:T(8,128)}, f32[2,512,128]{2,1,0:T(8,128)}, u32[]{:S(2)}, u32[]{:S(2)}) %collective-permute-start.4) | collective-permute-done | bytes 524320 | tf_op jit(solution)/shard_map/ppermute | solution.py:57
  50.7 1.6 %fusion.4 = f32[1,512,128]{2,1,0:T(8,128)S(1)} fusion(f32[2,512,128]{2,1,0:T(8,128)} %collective-permute-done.5, f32[2,512,128]{2,1,0:T(8,128)} %collective-permute-done.4, f32[2,512,128]{2,1,0:T(8,128)} %collective-permute-done.3, f32[2048,128]{1,0:T(8,128)} %collective-permute-done.2, s32[]{:T(128)S(6)} %select_n.393, ...), kind=kLoop, calls=%fused_computation.24 | loop fusion | flops 851968 | bytes 2889216 | tf_op jit(solution)/shard_map/stack | solution.py:367
  52.4 2.8 %collective-permute-start.6 = (f32[2,512,128]{2,1,0:T(8,128)S(1)}, f32[2,512,128]{2,1,0:T(8,128)S(1)}, u32[]{:S(2)}, u32[]{:S(2)}) collective-permute-start(f32[2,512,128]{2,1,0:T(8,128)S(1)} %pad_maximum_fusion.5), channel_id=1, source_target_pairs={{0,32},{1,9},{2,34},{3,11},{4,36},{5,13},{6,38},{7,15},{8,40},{9,1... | collective-permute-start | bytes 1572872 | tf_op jit(solution)/shard_map/ppermute | solution.py:57
  55.2 2.3 %collective-permute-start.8 = (f32[2,512,128]{2,1,0:T(8,128)S(1)}, f32[2,512,128]{2,1,0:T(8,128)S(1)}, u32[]{:S(2)}, u32[]{:S(2)}) collective-permute-start(f32[2,512,128]{2,1,0:T(8,128)S(1)} %pad_maximum_fusion.5), channel_id=1, source_target_pairs={{0,64},{1,17},{2,66},{3,19},{4,68},{5,21},{6,70},{7,23},{8,72},{9,... | collective-permute-start | bytes 1572872 | tf_op jit(solution)/shard_map/ppermute | solution.py:57
  58.5 3.4 %broadcast_select_fusion = f32[2,512,512]{2,1,0:T(8,128)} fusion(f32[2,512,512]{2,1,0:T(8,128)S(1)} %copy-done.2, f32[2,512,512]{2,1,0:T(8,128)} %collective-permute-done.11, pred[]{:T(512)S(6)} %eq.47), kind=kLoop, calls=%fused_computation.5 | loop fusion | flops 524288 | bytes 6291457 | tf_op jit(solution)/shard_map/jit(_where)/select_n | solution.py:332
  63.4 3.9 %collective-permute-done.8 = f32[2,512,128]{2,1,0:T(8,128)S(1)} collective-permute-done((f32[2,512,128]{2,1,0:T(8,128)S(1)}, f32[2,512,128]{2,1,0:T(8,128)S(1)}, u32[]{:S(2)}, u32[]{:S(2)}) %collective-permute-start.8) | collective-permute-done | bytes 524320 | tf_op jit(solution)/shard_map/ppermute | solution.py:57
  67.4 1.5 collective-permute-start.9
  72.0 1.6 copy-done.1
  73.6 2.0 %shard_map.42 = (bf16[1536,1024]{1,0:T(8,128)(2,1)S(1)}, bf16[1536,1024]{1,0:T(8,128)(2,1)S(1)}) custom-call(f32[2,512,512]{2,1,0:T(8,128)S(1)} %copy-done.1), custom_call_target="tpu_custom_call" | custom-call | flops 2000000000 | bytes 8388608 | tf_op jit(solution)/shard_map/pallas_call | solution.py:114
  75.6 23.4 %collective-permute-done.18 = f32[256,512]{1,0:T(8,128)} collective-permute-done((f32[256,512]{1,0:T(8,128)}, f32[256,512]{1,0:T(8,128)}, u32[]{:S(2)}, u32[]{:S(2)}) %collective-permute-start.18) | collective-permute-done | bytes 524320 | tf_op jit(solution)/shard_map/ppermute | solution.py:57
  100.3 2.4 %select_select_fusion.mine_ref = f32[2,512,512]{2,1,0:T(8,128)S(1)} fusion(f32[2,512,512]{2,1,0:T(8,128)S(1)} %copy-done.3, f32[2,512,512]{2,1,0:T(8,128)} %collective-permute-done.11, f32[2,512,512]{2,1,0:T(8,128)} %collective-permute-done.12, pred[]{:T(512)S(6)} %eq.48, pred[]{:T(512)S(6)} %eq.47), kind=kLoop, calls=%fused_computation.1 | loop fusion | flops 1048576 | bytes 8388610 | tf_op jit(solution)/shard_map/jit(_where)/select_n | solution.py:67
  102.9 12.9 %collective-permute-start.19 = (f32[1280,512]{1,0:T(8,128)S(1)}, f32[1280,512]{1,0:T(8,128)S(1)}, u32[]{:S(2)}, u32[]{:S(2)}) collective-permute-start(f32[1280,512]{1,0:T(8,128)S(1)} %pad_maximum_fusion), channel_id=1, source_target_pairs={{0,1},{1,0},{2,3},{3,2},{4,5},{5,4},{6,7},{7,6},{8,9},{9,8},{10,11... | collective-permute-start | bytes 7864328 | tf_op jit(solution)/shard_map/ppermute | solution.py:57
  118.7 2.9 %collective-permute-start.21 = (f32[2048,128]{1,0:T(8,128)S(1)}, f32[2048,128]{1,0:T(8,128)S(1)}, u32[]{:S(2)}, u32[]{:S(2)}) collective-permute-start(f32[2048,128]{1,0:T(8,128)S(1)} %slice_bitcast_fusion), channel_id=1, source_target_pairs={{0,24},{1,97},{2,26},{3,99},{4,28},{5,101},{6,30},{7,103},{8,0},{9... | collective-permute-start | bytes 3145736 | tf_op jit(solution)/shard_map/ppermute | solution.py:57
  121.9 15.7 %shard_map.44 = (f32[2,2,512,512]{3,2,1,0:T(8,128)}, bf16[4,1024,256]{2,1,0:T(8,128)(2,1)S(1)}, bf16[4,1024,256]{2,1,0:T(8,128)(2,1)S(1)}, bf16[4,1024,256]{2,1,0:T(8,128)(2,1)S(1)}, bf16[4,1024,256]{2,1,0:T(8,128)(2,1)S(1)}) custom-call(s32[3]{0:T(128)S(1)} %pad_add_fusion.where_ref, f32[2,512,512]{2,1,0:T(8,128)S(1)} %select_select_fusion.mine_ref, ...), custom_call_target="tpu_custom_call" | custom-call | flops 11000000512 | bytes 25165824 | tf_op jit(solution)/shard_map/pallas_call | solution.py:169
  137.6 25.0 %shard_map.45 = f32[16384,128]{1,0:T(8,128)} custom-call(s32[4]{0:T(128)S(1)} %and_select_fusion.ks_ref, f32[16384,128]{1,0:T(8,128)} %bitcast.90, bf16[4,1024,256]{2,1,0:T(8,128)(2,1)S(1)} %get-tuple-element.32.rest_0_.rest_4_.rest_8_.rest_12_, bf16[4,1024,256]{2,1,0:T(8,128)(2,1)S(1)} %get-tuple-element.33.rest_1_.rest_5_.rest_9_.rest_13_, ...), custom_call_target="tpu_custom_call" | custom-call | flops 13200000000 | bytes 33554432 | tf_op jit(solution)/shard_map/pallas_call | solution.py:247
  (62 shorter events, 22.1 us)
Async XLA Ops:
  4.4 17.4 %collective-permute-start = (f32[2048,128]{1,0:T(8,128)}, f32[2048,128]{1,0:T(8,128)S(1)}, u32[]{:S(2)}, u32[]{:S(2)}) collective-permute-start(f32[2048,128]{1,0:T(8,128)} %get-tuple-element.44), channel_id=1, source_target_pairs={{0,8},{1,33},{2,10},{3,35},{4,12},{5,37},{6,14},{7,39},{8,16},{9,4... | collective-permute-start | bytes 3145736 | tf_op jit(solution)/shard_map/ppermute | solution.py:57
  5.1 16.7 %collective-permute-start.1 = (f32[2048,128]{1,0:T(8,128)}, f32[2048,128]{1,0:T(8,128)S(1)}, u32[]{:S(2)}, u32[]{:S(2)}) collective-permute-start(f32[2048,128]{1,0:T(8,128)} %get-tuple-element.46), channel_id=1, source_target_pairs={{0,16},{1,65},{2,18},{3,67},{4,20},{5,69},{6,22},{7,71},{8,24},{9,... | collective-permute-start | bytes 3145736 | tf_op jit(solution)/shard_map/ppermute | solution.py:57
  5.8 16.0 %collective-permute-start.2 = (f32[2048,128]{1,0:T(8,128)}, f32[2048,128]{1,0:T(8,128)}, u32[]{:S(2)}, u32[]{:S(2)}) collective-permute-start(f32[2048,128]{1,0:T(8,128)} %get-tuple-element.45), channel_id=1, source_target_pairs={{0,24},{1,97},{2,26},{3,99},{4,28},{5,101},{6,30},{7,103},{8,0},{9... | collective-permute-start | bytes 3145736 | tf_op jit(solution)/shard_map/ppermute | solution.py:57
  11.2 8.3 %collective-permute-start.13 = (f32[256,512]{1,0:T(8,128)S(1)}, f32[256,512]{1,0:T(8,128)S(1)}, u32[]{:S(2)}, u32[]{:S(2)}) collective-permute-start(f32[256,512]{1,0:T(8,128)S(1)} %shard_map.43), channel_id=1, source_target_pairs={{1,9},{8,40}} | collective-permute-start | bytes 1572872 | tf_op jit(solution)/shard_map/ppermute | solution.py:57
  17.4 41.1 %collective-permute-start.11 = (f32[2,512,512]{2,1,0:T(8,128)}, f32[2,512,512]{2,1,0:T(8,128)}, u32[]{:S(2)}, u32[]{:S(2)}) collective-permute-start(f32[2,512,512]{2,1,0:T(8,128)} %shard_map.41), channel_id=1, source_target_pairs={{0,2},{1,7},{8,10},{9,15},{16,18},{17,23},{24,26},{25,31},{32,34},... | collective-permute-start | bytes 6291464 | tf_op jit(solution)/shard_map/ppermute | solution.py:57
  20.3 9.7 %collective-permute-start.14 = (f32[256,512]{1,0:T(8,128)}, f32[256,512]{1,0:T(8,128)}, u32[]{:S(2)}, u32[]{:S(2)}) collective-permute-start(f32[256,512]{1,0:T(8,128)} %broadcast_select_fusion.1), channel_id=1, source_target_pairs={{1,25},{8,104},{9,17},{40,72}} | collective-permute-start | bytes 1572872 | tf_op jit(solution)/shard_map/ppermute | solution.py:57
  24.3 18.3 %collective-permute-start.3 = (f32[2,512,128]{2,1,0:T(8,128)}, f32[2,512,128]{2,1,0:T(8,128)}, u32[]{:S(2)}, u32[]{:S(2)}) collective-permute-start(f32[2,512,128]{2,1,0:T(8,128)} %pad_maximum_fusion.2), channel_id=1, source_target_pairs={{0,32},{1,9},{2,34},{3,11},{4,36},{5,13},{6,38},{7,15},{8,40},{9,1... | collective-permute-start | bytes 1572872 | tf_op jit(solution)/shard_map/ppermute | solution.py:57
  26.4 23.0 %collective-permute-start.4 = (f32[2,512,128]{2,1,0:T(8,128)}, f32[2,512,128]{2,1,0:T(8,128)}, u32[]{:S(2)}, u32[]{:S(2)}) collective-permute-start(f32[2,512,128]{2,1,0:T(8,128)} %pad_maximum_fusion.3), channel_id=1, source_target_pairs={{0,64},{1,17},{2,66},{3,19},{4,68},{5,21},{6,70},{7,23},{8,72},{9,... | collective-permute-start | bytes 1572872 | tf_op jit(solution)/shard_map/ppermute | solution.py:57
  28.5 20.8 %collective-permute-start.5 = (f32[2,512,128]{2,1,0:T(8,128)}, f32[2,512,128]{2,1,0:T(8,128)}, u32[]{:S(2)}, u32[]{:S(2)}) collective-permute-start(f32[2,512,128]{2,1,0:T(8,128)} %pad_maximum_fusion.4), channel_id=1, source_target_pairs={{0,96},{1,25},{2,98},{3,27},{4,100},{5,29},{6,102},{7,31},{8,104},... | collective-permute-start | bytes 1572872 | tf_op jit(solution)/shard_map/ppermute | solution.py:57
  31.2 26.3 %collective-permute-start.15 = (f32[256,512]{1,0:T(8,128)S(1)}, f32[256,512]{1,0:T(8,128)S(1)}, u32[]{:S(2)}, u32[]{:S(2)}) collective-permute-start(f32[256,512]{1,0:T(8,128)S(1)} %select_select_fusion.3), channel_id=1, source_target_pairs={{1,33},{8,16},{9,41},{17,49},{25,57},{40,48},{72,80},{104,112}} | collective-permute-start | bytes 1572872 | tf_op jit(solution)/shard_map/ppermute | solution.py:57
  52.4 6.1 %copy-start.2 = (f32[2,512,512]{2,1,0:T(8,128)S(1)}, f32[2,512,512]{2,1,0:T(8,128)}, u32[]{:S(2)}) copy-start(f32[2,512,512]{2,1,0:T(8,128)} %shard_map.41) | copy-start | bytes 6291460
  52.4 10.8 %collective-permute-start.6 = (f32[2,512,128]{2,1,0:T(8,128)S(1)}, f32[2,512,128]{2,1,0:T(8,128)S(1)}, u32[]{:S(2)}, u32[]{:S(2)}) collective-permute-start(f32[2,512,128]{2,1,0:T(8,128)S(1)} %pad_maximum_fusion.5), channel_id=1, source_target_pairs={{0,32},{1,9},{2,34},{3,11},{4,36},{5,13},{6,38},{7,15},{8,40},{9,1... | collective-permute-start | bytes 1572872 | tf_op jit(solution)/shard_map/ppermute | solution.py:57
  55.2 8.1 %collective-permute-start.7 = (f32[2,512,128]{2,1,0:T(8,128)S(1)}, f32[2,512,128]{2,1,0:T(8,128)S(1)}, u32[]{:S(2)}, u32[]{:S(2)}) collective-permute-start(f32[2,512,128]{2,1,0:T(8,128)S(1)} %pad_maximum_fusion.5), channel_id=1, source_target_pairs={{0,96},{1,25},{2,98},{3,27},{4,100},{5,29},{6,102},{7,31},{8,104},... | collective-permute-start | bytes 1572872 | tf_op jit(solution)/shard_map/ppermute | solution.py:57
  55.2 12.1 %collective-permute-start.8 = (f32[2,512,128]{2,1,0:T(8,128)S(1)}, f32[2,512,128]{2,1,0:T(8,128)S(1)}, u32[]{:S(2)}, u32[]{:S(2)}) collective-permute-start(f32[2,512,128]{2,1,0:T(8,128)S(1)} %pad_maximum_fusion.5), channel_id=1, source_target_pairs={{0,64},{1,17},{2,66},{3,19},{4,68},{5,21},{6,70},{7,23},{8,72},{9,... | collective-permute-start | bytes 1572872 | tf_op jit(solution)/shard_map/ppermute | solution.py:57
  57.6 11.3 %collective-permute-start.16 = (f32[256,512]{1,0:T(8,128)S(1)}, f32[256,512]{1,0:T(8,128)S(1)}, u32[]{:S(2)}, u32[]{:S(2)}) collective-permute-start(f32[256,512]{1,0:T(8,128)S(1)} %broadcast_select_fusion.2), channel_id=1, source_target_pairs={{1,97},{8,0},{9,105},{16,24},{17,113},{25,121},{33,65},{40,32},{41... | collective-permute-start | bytes 1572872 | tf_op jit(solution)/shard_map/ppermute | solution.py:57
  61.9 38.3 %collective-permute-start.12 = (f32[2,512,512]{2,1,0:T(8,128)}, f32[2,512,512]{2,1,0:T(8,128)}, u32[]{:S(2)}, u32[]{:S(2)}) collective-permute-start(f32[2,512,512]{2,1,0:T(8,128)} %broadcast_select_fusion), channel_id=1, source_target_pairs={{0,6},{1,3},{2,4},{7,5},{8,14},{9,11},{10,12},{15,13},{16,22},{17,... | collective-permute-start | bytes 6291464 | tf_op jit(solution)/shard_map/ppermute | solution.py:57
  67.4 35.3 %collective-permute-start.10 = (f32[2,2048,128]{2,1,0:T(8,128)S(1)}, f32[2,2048,128]{2,1,0:T(8,128)}, u32[]{:S(2)}, u32[]{:S(2)}) collective-permute-start(f32[2,2048,128]{2,1,0:T(8,128)S(1)} %bitcast.92), channel_id=1, source_target_pairs={{0,24},{1,97},{2,26},{3,99},{4,28},{5,101},{6,30},{7,103},{8,0},{9... | collective-permute-start | bytes 6291464 | tf_op jit(solution)/shard_map/ppermute | solution.py:57
  67.4 35.2 %collective-permute-start.9 = (f32[2,2048,128]{2,1,0:T(8,128)S(1)}, f32[2,2048,128]{2,1,0:T(8,128)}, u32[]{:S(2)}, u32[]{:S(2)}) collective-permute-start(f32[2,2048,128]{2,1,0:T(8,128)S(1)} %bitcast.93), channel_id=1, source_target_pairs={{0,8},{1,33},{2,10},{3,35},{4,12},{5,37},{6,14},{7,39},{8,16},{9,4... | collective-permute-start | bytes 6291464 | tf_op jit(solution)/shard_map/ppermute | solution.py:57
  69.0 0.7 collective-permute-start.17
  70.7 28.3 %collective-permute-start.18 = (f32[256,512]{1,0:T(8,128)}, f32[256,512]{1,0:T(8,128)}, u32[]{:S(2)}, u32[]{:S(2)}) collective-permute-start(f32[256,512]{1,0:T(8,128)} %broadcast_select_fusion.3), channel_id=1, source_target_pairs={{0,6},{1,3},{2,4},{7,5},{8,14},{9,11},{10,12},{15,13},{16,22},{17,... | collective-permute-start | bytes 1572872 | tf_op jit(solution)/shard_map/ppermute | solution.py:57
  75.6 24.7 %copy-start.3 = (f32[2,512,512]{2,1,0:T(8,128)S(1)}, f32[2,512,512]{2,1,0:T(8,128)}, u32[]{:S(2)}) copy-start(f32[2,512,512]{2,1,0:T(8,128)} %shard_map.41) | copy-start | bytes 6291460
  102.9 18.6 %collective-permute-start.19 = (f32[1280,512]{1,0:T(8,128)S(1)}, f32[1280,512]{1,0:T(8,128)S(1)}, u32[]{:S(2)}, u32[]{:S(2)}) collective-permute-start(f32[1280,512]{1,0:T(8,128)S(1)} %pad_maximum_fusion), channel_id=1, source_target_pairs={{0,1},{1,0},{2,3},{3,2},{4,5},{5,4},{6,7},{7,6},{8,9},{9,8},{10,11... | collective-permute-start | bytes 7864328 | tf_op jit(solution)/shard_map/ppermute | solution.py:57
  117.3 20.3 %collective-permute-start.20 = (f32[2048,128]{1,0:T(8,128)S(1)}, f32[2048,128]{1,0:T(8,128)S(1)}, u32[]{:S(2)}, u32[]{:S(2)}) collective-permute-start(f32[2048,128]{1,0:T(8,128)S(1)} %slice_bitcast_fusion.1), channel_id=1, source_target_pairs={{0,8},{1,33},{2,10},{3,35},{4,12},{5,37},{6,14},{7,39},{8,16},{9,4... | collective-permute-start | bytes 3145736 | tf_op jit(solution)/shard_map/ppermute | solution.py:57
  118.7 18.9 %collective-permute-start.21 = (f32[2048,128]{1,0:T(8,128)S(1)}, f32[2048,128]{1,0:T(8,128)S(1)}, u32[]{:S(2)}, u32[]{:S(2)}) collective-permute-start(f32[2048,128]{1,0:T(8,128)S(1)} %slice_bitcast_fusion), channel_id=1, source_target_pairs={{0,24},{1,97},{2,26},{3,99},{4,28},{5,101},{6,30},{7,103},{8,0},{9... | collective-permute-start | bytes 3145736 | tf_op jit(solution)/shard_map/ppermute | solution.py:57
  (2 other events, 5.0 us)

commit v5 on v4

--- a/solution.py
+++ b/solution.py
@@ -13,6 +13,7 @@
 SPLIT = 2
 VMEM_BYTES = 36 * 1024 * 1024
 SMALL_VMEM_BYTES = 24 * 1024 * 1024
+EARLY_VMEM_BYTES = 16 * 1024 * 1024
 
 
 def place(z, y, x, c):
@@ -115,7 +116,7 @@
         weights_kernel,
         out_shape=[jax.ShapeDtypeStruct((3 * nb, 2 * nb), jnp.bfloat16)] * 2,
         scratch_shapes=[pltpu.VMEM((3 * nb, nb), jnp.bfloat16)],
-        compiler_params=pltpu.CompilerParams(vmem_limit_bytes=SMALL_VMEM_BYTES),
+        compiler_params=pltpu.CompilerParams(vmem_limit_bytes=EARLY_VMEM_BYTES),
         cost_estimate=pl.CostEstimate(flops=2 * 10**9, bytes_accessed=8 * 2**20, transcendentals=0),
     )(inverse_factors)
 
@@ -310,7 +311,7 @@
         ],
         out_specs=pl.BlockSpec((nb // 2, nb), lambda i: (0, 0)),
         out_shape=jax.ShapeDtypeStruct((nb // 2, nb), lines.dtype),
-        compiler_params=pltpu.CompilerParams(vmem_limit_bytes=SMALL_VMEM_BYTES),
+        compiler_params=pltpu.CompilerParams(vmem_limit_bytes=EARLY_VMEM_BYTES),
         cost_estimate=pl.CostEstimate(flops=0, bytes_accessed=5 * 2**20, transcendentals=0),
     )(core, lines)
 

time: 163 us -> 163 us (level)
  no operation moved by 1% of the time
where the time goes in v5:
time: 163 us
  Pallas kernels  48.6 us (30%)
  waiting for transfers between devices  45 us (28%)
  starting transfers between devices  38.4 us (24%)
  other arithmetic  18 us (11%)
  local copies, waits for them, and re-layouts  11.6 us (7%)
    ppermute x22, waiting for transfers between devices, send(): return lax.ppermute(x, AXES, moves)  45 us
    ppermute x22, starting transfers between devices, send(): return lax.ppermute(x, AXES, moves)  38.4 us
    pallas_call x1, Pallas kernels, subtract_products(): pl.pallas_call(functools.partial(update_kernel, count), grid_spec=pltpu.P...  25 us
    pallas_call x1, Pallas kernels, row_factors(): pl.pallas_call(factors_kernel, grid=(rbd, SPLIT), in_specs=[pl.BlockSpec(...  15.7 us
    pallas_call x1, Pallas kernels, first_column(): pl.pallas_call(column_kernel, grid=(rbd, 2), in_specs=[pl.BlockSpec((tile...  5.56 us
    select_n x4, other arithmetic, share(): two = send(jnp.where(index == 0, x, one), second)  5.32 us
    unnamed x8, local copies, waits for them, and re-layouts  4.98 us
    select_n x4, other arithmetic, choose(): result = jnp.where(index == i, options[i], result)  4.88 us
  transfers between devices with their start and end apart: 22, of which 5 were waited for; matrix products, arithmetic and copies ran while one was open for 13% of the time, Pallas kernels for 14%

profile of v5, /device:TPU:21, one launch (start us, length us, event | category | flops | bytes accessed | tf_op | source)
XLA Modules:
  0.0 162.7 jit_solution(13130078688521806168)
XLA Ops:
  0.7 3.6 %constant_dynamic-slice_fusion.2 = (f32[2048,128]{1,0:T(8,128)}, f32[2048,128]{1,0:T(8,128)}, f32[2048,128]{1,0:T(8,128)}) fusion(f32[16384,128]{1,0:T(8,128)} %bitcast.85, s32[]{:T(128)S(6)} %select_n.400, s32[]{:T(128)S(6)} %select_n.405, s32[]{:T(128)S(6)} %select_n.403), kind=kLoop, calls=%fused_computation.41 | loop fusion | bytes 6291468 | tf_op jit(solution)/shard_map/dynamic_slice | solution.py:342
  5.8 1.6 %collective-permute-start.2 = (f32[2048,128]{1,0:T(8,128)}, f32[2048,128]{1,0:T(8,128)}, u32[]{:S(2)}, u32[]{:S(2)}) collective-permute-start(f32[2048,128]{1,0:T(8,128)} %get-tuple-element.45), channel_id=1, source_target_pairs={{0,24},{1,97},{2,26},{3,99},{4,28},{5,101},{6,30},{7,103},{8,0},{9... | collective-permute-start | bytes 3145736 | tf_op jit(solution)/shard_map/ppermute | solution.py:58
  7.5 3.4 %copy-done = f32[2,512,4,512]{3,2,1,0:T(4,128)S(1)} copy-done((f32[2,512,4,512]{3,2,1,0:T(4,128)S(1)}, f32[2,512,4,512]{3,2,1,0:T(4,128)}, u32[]{:S(2)}) %copy-start) | copy-done | bytes 8388632
  11.9 5.6 %shard_map.41 = f32[2,512,512]{2,1,0:T(8,128)} custom-call(f32[16384,128]{1,0:T(8,128)} %bitcast.86), custom_call_target="tpu_custom_call" | custom-call | bytes 10485760 | tf_op jit(solution)/shard_map/pallas_call | solution.py:276
  17.4 2.0 %collective-permute-start.11 = (f32[2,512,512]{2,1,0:T(8,128)}, f32[2,512,512]{2,1,0:T(8,128)}, u32[]{:S(2)}, u32[]{:S(2)}) collective-permute-start(f32[2,512,512]{2,1,0:T(8,128)} %shard_map.41), channel_id=1, source_target_pairs={{0,2},{1,7},{8,10},{9,15},{16,18},{17,23},{24,26},{25,31},{32,34},... | collective-permute-start | bytes 6291464 | tf_op jit(solution)/shard_map/ppermute | solution.py:58
  20.3 1.5 collective-permute-start.14
  21.8 1.6 select_bitcast_fusion.6
  28.5 1.5 collective-permute-start.5
  31.9 10.7 %collective-permute-done.3 = f32[2,512,128]{2,1,0:T(8,128)} collective-permute-done((f32[2,512,128]{2,1,0:T(8,128)}, f32[2,512,128]{2,1,0:T(8,128)}, u32[]{:S(2)}, u32[]{:S(2)}) %collective-permute-start.3) | collective-permute-done | bytes 524320 | tf_op jit(solution)/shard_map/ppermute | solution.py:58
  42.6 6.8 %collective-permute-done.4 = f32[2,512,128]{2,1,0:T(8,128)} collective-permute-done((f32[2,512,128]{2,1,0:T(8,128)}, f32[2,512,128]{2,1,0:T(8,128)}, u32[]{:S(2)}, u32[]{:S(2)}) %collective-permute-start.4) | collective-permute-done | bytes 524320 | tf_op jit(solution)/shard_map/ppermute | solution.py:58
  50.7 1.6 %fusion.4 = f32[1,512,128]{2,1,0:T(8,128)S(1)} fusion(f32[2,512,128]{2,1,0:T(8,128)} %collective-permute-done.5, f32[2,512,128]{2,1,0:T(8,128)} %collective-permute-done.4, f32[2,512,128]{2,1,0:T(8,128)} %collective-permute-done.3, f32[2048,128]{1,0:T(8,128)} %collective-permute-done.2, s32[]{:T(128)S(6)} %select_n.393, ...), kind=kLoop, calls=%fused_computation.24 | loop fusion | flops 851968 | bytes 2889216 | tf_op jit(solution)/shard_map/stack | solution.py:368
  52.4 2.8 %collective-permute-start.6 = (f32[2,512,128]{2,1,0:T(8,128)S(1)}, f32[2,512,128]{2,1,0:T(8,128)S(1)}, u32[]{:S(2)}, u32[]{:S(2)}) collective-permute-start(f32[2,512,128]{2,1,0:T(8,128)S(1)} %pad_maximum_fusion.5), channel_id=1, source_target_pairs={{0,32},{1,9},{2,34},{3,11},{4,36},{5,13},{6,38},{7,15},{8,40},{9,1... | collective-permute-start | bytes 1572872 | tf_op jit(solution)/shard_map/ppermute | solution.py:58
  55.2 2.3 %collective-permute-start.8 = (f32[2,512,128]{2,1,0:T(8,128)S(1)}, f32[2,512,128]{2,1,0:T(8,128)S(1)}, u32[]{:S(2)}, u32[]{:S(2)}) collective-permute-start(f32[2,512,128]{2,1,0:T(8,128)S(1)} %pad_maximum_fusion.5), channel_id=1, source_target_pairs={{0,64},{1,17},{2,66},{3,19},{4,68},{5,21},{6,70},{7,23},{8,72},{9,... | collective-permute-start | bytes 1572872 | tf_op jit(solution)/shard_map/ppermute | solution.py:58
  58.5 3.4 %broadcast_select_fusion = f32[2,512,512]{2,1,0:T(8,128)} fusion(f32[2,512,512]{2,1,0:T(8,128)S(1)} %copy-done.2, f32[2,512,512]{2,1,0:T(8,128)} %collective-permute-done.11, pred[]{:T(512)S(6)} %eq.47), kind=kLoop, calls=%fused_computation.5 | loop fusion | flops 524288 | bytes 6291457 | tf_op jit(solution)/shard_map/jit(_where)/select_n | solution.py:333
  63.4 3.9 %collective-permute-done.8 = f32[2,512,128]{2,1,0:T(8,128)S(1)} collective-permute-done((f32[2,512,128]{2,1,0:T(8,128)S(1)}, f32[2,512,128]{2,1,0:T(8,128)S(1)}, u32[]{:S(2)}, u32[]{:S(2)}) %collective-permute-start.8) | collective-permute-done | bytes 524320 | tf_op jit(solution)/shard_map/ppermute | solution.py:58
  67.4 1.5 collective-permute-start.9
  72.0 1.6 copy-done.1
  73.6 2.0 %shard_map.42 = (bf16[1536,1024]{1,0:T(8,128)(2,1)S(1)}, bf16[1536,1024]{1,0:T(8,128)(2,1)S(1)}) custom-call(f32[2,512,512]{2,1,0:T(8,128)S(1)} %copy-done.1), custom_call_target="tpu_custom_call" | custom-call | flops 2000000000 | bytes 8388608 | tf_op jit(solution)/shard_map/pallas_call | solution.py:115
  75.6 23.4 %collective-permute-done.18 = f32[256,512]{1,0:T(8,128)} collective-permute-done((f32[256,512]{1,0:T(8,128)}, f32[256,512]{1,0:T(8,128)}, u32[]{:S(2)}, u32[]{:S(2)}) %collective-permute-start.18) | collective-permute-done | bytes 524320 | tf_op jit(solution)/shard_map/ppermute | solution.py:58
  100.3 2.4 %select_select_fusion.mine_ref = f32[2,512,512]{2,1,0:T(8,128)S(1)} fusion(f32[2,512,512]{2,1,0:T(8,128)S(1)} %copy-done.3, f32[2,512,512]{2,1,0:T(8,128)} %collective-permute-done.11, f32[2,512,512]{2,1,0:T(8,128)} %collective-permute-done.12, pred[]{:T(512)S(6)} %eq.48, pred[]{:T(512)S(6)} %eq.47), kind=kLoop, calls=%fused_computation.1 | loop fusion | flops 1048576 | bytes 8388610 | tf_op jit(solution)/shard_map/jit(_where)/select_n | solution.py:68
  102.9 12.9 %collective-permute-start.19 = (f32[1280,512]{1,0:T(8,128)S(1)}, f32[1280,512]{1,0:T(8,128)S(1)}, u32[]{:S(2)}, u32[]{:S(2)}) collective-permute-start(f32[1280,512]{1,0:T(8,128)S(1)} %pad_maximum_fusion), channel_id=1, source_target_pairs={{0,1},{1,0},{2,3},{3,2},{4,5},{5,4},{6,7},{7,6},{8,9},{9,8},{10,11... | collective-permute-start | bytes 7864328 | tf_op jit(solution)/shard_map/ppermute | solution.py:58
  118.7 2.9 %collective-permute-start.21 = (f32[2048,128]{1,0:T(8,128)S(1)}, f32[2048,128]{1,0:T(8,128)S(1)}, u32[]{:S(2)}, u32[]{:S(2)}) collective-permute-start(f32[2048,128]{1,0:T(8,128)S(1)} %slice_bitcast_fusion), channel_id=1, source_target_pairs={{0,24},{1,97},{2,26},{3,99},{4,28},{5,101},{6,30},{7,103},{8,0},{9... | collective-permute-start | bytes 3145736 | tf_op jit(solution)/shard_map/ppermute | solution.py:58
  121.9 15.7 %shard_map.44 = (f32[2,2,512,512]{3,2,1,0:T(8,128)}, bf16[4,1024,256]{2,1,0:T(8,128)(2,1)S(1)}, bf16[4,1024,256]{2,1,0:T(8,128)(2,1)S(1)}, bf16[4,1024,256]{2,1,0:T(8,128)(2,1)S(1)}, bf16[4,1024,256]{2,1,0:T(8,128)(2,1)S(1)}) custom-call(s32[3]{0:T(128)S(1)} %pad_add_fusion.where_ref, f32[2,512,512]{2,1,0:T(8,128)S(1)} %select_select_fusion.mine_ref, ...), custom_call_target="tpu_custom_call" | custom-call | flops 11000000512 | bytes 25165824 | tf_op jit(solution)/shard_map/pallas_call | solution.py:170
  137.6 25.0 %shard_map.45 = f32[16384,128]{1,0:T(8,128)} custom-call(s32[4]{0:T(128)S(1)} %and_select_fusion.ks_ref, f32[16384,128]{1,0:T(8,128)} %bitcast.90, bf16[4,1024,256]{2,1,0:T(8,128)(2,1)S(1)} %get-tuple-element.32.rest_0_.rest_4_.rest_8_.rest_12_, bf16[4,1024,256]{2,1,0:T(8,128)(2,1)S(1)} %get-tuple-element.33.rest_1_.rest_5_.rest_9_.rest_13_, ...), custom_call_target="tpu_custom_call" | custom-call | flops 13200000000 | bytes 33554432 | tf_op jit(solution)/shard_map/pallas_call | solution.py:248
  (62 shorter events, 22.1 us)
Async XLA Ops:
  4.4 17.4 %collective-permute-start = (f32[2048,128]{1,0:T(8,128)}, f32[2048,128]{1,0:T(8,128)S(1)}, u32[]{:S(2)}, u32[]{:S(2)}) collective-permute-start(f32[2048,128]{1,0:T(8,128)} %get-tuple-element.44), channel_id=1, source_target_pairs={{0,8},{1,33},{2,10},{3,35},{4,12},{5,37},{6,14},{7,39},{8,16},{9,4... | collective-permute-start | bytes 3145736 | tf_op jit(solution)/shard_map/ppermute | solution.py:58
  5.1 16.7 %collective-permute-start.1 = (f32[2048,128]{1,0:T(8,128)}, f32[2048,128]{1,0:T(8,128)S(1)}, u32[]{:S(2)}, u32[]{:S(2)}) collective-permute-start(f32[2048,128]{1,0:T(8,128)} %get-tuple-element.46), channel_id=1, source_target_pairs={{0,16},{1,65},{2,18},{3,67},{4,20},{5,69},{6,22},{7,71},{8,24},{9,... | collective-permute-start | bytes 3145736 | tf_op jit(solution)/shard_map/ppermute | solution.py:58
  5.8 16.0 %collective-permute-start.2 = (f32[2048,128]{1,0:T(8,128)}, f32[2048,128]{1,0:T(8,128)}, u32[]{:S(2)}, u32[]{:S(2)}) collective-permute-start(f32[2048,128]{1,0:T(8,128)} %get-tuple-element.45), channel_id=1, source_target_pairs={{0,24},{1,97},{2,26},{3,99},{4,28},{5,101},{6,30},{7,103},{8,0},{9... | collective-permute-start | bytes 3145736 | tf_op jit(solution)/shard_map/ppermute | solution.py:58
  11.2 8.3 %collective-permute-start.13 = (f32[256,512]{1,0:T(8,128)S(1)}, f32[256,512]{1,0:T(8,128)S(1)}, u32[]{:S(2)}, u32[]{:S(2)}) collective-permute-start(f32[256,512]{1,0:T(8,128)S(1)} %shard_map.43), channel_id=1, source_target_pairs={{1,9},{8,40}} | collective-permute-start | bytes 1572872 | tf_op jit(solution)/shard_map/ppermute | solution.py:58
  17.4 41.1 %collective-permute-start.11 = (f32[2,512,512]{2,1,0:T(8,128)}, f32[2,512,512]{2,1,0:T(8,128)}, u32[]{:S(2)}, u32[]{:S(2)}) collective-permute-start(f32[2,512,512]{2,1,0:T(8,128)} %shard_map.41), channel_id=1, source_target_pairs={{0,2},{1,7},{8,10},{9,15},{16,18},{17,23},{24,26},{25,31},{32,34},... | collective-permute-start | bytes 6291464 | tf_op jit(solution)/shard_map/ppermute | solution.py:58
  20.3 9.7 %collective-permute-start.14 = (f32[256,512]{1,0:T(8,128)}, f32[256,512]{1,0:T(8,128)}, u32[]{:S(2)}, u32[]{:S(2)}) collective-permute-start(f32[256,512]{1,0:T(8,128)} %broadcast_select_fusion.1), channel_id=1, source_target_pairs={{1,25},{8,104},{9,17},{40,72}} | collective-permute-start | bytes 1572872 | tf_op jit(solution)/shard_map/ppermute | solution.py:58
  24.3 18.3 %collective-permute-start.3 = (f32[2,512,128]{2,1,0:T(8,128)}, f32[2,512,128]{2,1,0:T(8,128)}, u32[]{:S(2)}, u32[]{:S(2)}) collective-permute-start(f32[2,512,128]{2,1,0:T(8,128)} %pad_maximum_fusion.2), channel_id=1, source_target_pairs={{0,32},{1,9},{2,34},{3,11},{4,36},{5,13},{6,38},{7,15},{8,40},{9,1... | collective-permute-start | bytes 1572872 | tf_op jit(solution)/shard_map/ppermute | solution.py:58
  26.4 23.0 %collective-permute-start.4 = (f32[2,512,128]{2,1,0:T(8,128)}, f32[2,512,128]{2,1,0:T(8,128)}, u32[]{:S(2)}, u32[]{:S(2)}) collective-permute-start(f32[2,512,128]{2,1,0:T(8,128)} %pad_maximum_fusion.3), channel_id=1, source_target_pairs={{0,64},{1,17},{2,66},{3,19},{4,68},{5,21},{6,70},{7,23},{8,72},{9,... | collective-permute-start | bytes 1572872 | tf_op jit(solution)/shard_map/ppermute | solution.py:58
  28.5 20.8 %collective-permute-start.5 = (f32[2,512,128]{2,1,0:T(8,128)}, f32[2,512,128]{2,1,0:T(8,128)}, u32[]{:S(2)}, u32[]{:S(2)}) collective-permute-start(f32[2,512,128]{2,1,0:T(8,128)} %pad_maximum_fusion.4), channel_id=1, source_target_pairs={{0,96},{1,25},{2,98},{3,27},{4,100},{5,29},{6,102},{7,31},{8,104},... | collective-permute-start | bytes 1572872 | tf_op jit(solution)/shard_map/ppermute | solution.py:58
  31.2 26.3 %collective-permute-start.15 = (f32[256,512]{1,0:T(8,128)S(1)}, f32[256,512]{1,0:T(8,128)S(1)}, u32[]{:S(2)}, u32[]{:S(2)}) collective-permute-start(f32[256,512]{1,0:T(8,128)S(1)} %select_select_fusion.3), channel_id=1, source_target_pairs={{1,33},{8,16},{9,41},{17,49},{25,57},{40,48},{72,80},{104,112}} | collective-permute-start | bytes 1572872 | tf_op jit(solution)/shard_map/ppermute | solution.py:58
  52.4 6.1 %copy-start.2 = (f32[2,512,512]{2,1,0:T(8,128)S(1)}, f32[2,512,512]{2,1,0:T(8,128)}, u32[]{:S(2)}) copy-start(f32[2,512,512]{2,1,0:T(8,128)} %shard_map.41) | copy-start | bytes 6291460
  52.4 10.8 %collective-permute-start.6 = (f32[2,512,128]{2,1,0:T(8,128)S(1)}, f32[2,512,128]{2,1,0:T(8,128)S(1)}, u32[]{:S(2)}, u32[]{:S(2)}) collective-permute-start(f32[2,512,128]{2,1,0:T(8,128)S(1)} %pad_maximum_fusion.5), channel_id=1, source_target_pairs={{0,32},{1,9},{2,34},{3,11},{4,36},{5,13},{6,38},{7,15},{8,40},{9,1... | collective-permute-start | bytes 1572872 | tf_op jit(solution)/shard_map/ppermute | solution.py:58
  55.2 8.1 %collective-permute-start.7 = (f32[2,512,128]{2,1,0:T(8,128)S(1)}, f32[2,512,128]{2,1,0:T(8,128)S(1)}, u32[]{:S(2)}, u32[]{:S(2)}) collective-permute-start(f32[2,512,128]{2,1,0:T(8,128)S(1)} %pad_maximum_fusion.5), channel_id=1, source_target_pairs={{0,96},{1,25},{2,98},{3,27},{4,100},{5,29},{6,102},{7,31},{8,104},... | collective-permute-start | bytes 1572872 | tf_op jit(solution)/shard_map/ppermute | solution.py:58
  55.2 12.1 %collective-permute-start.8 = (f32[2,512,128]{2,1,0:T(8,128)S(1)}, f32[2,512,128]{2,1,0:T(8,128)S(1)}, u32[]{:S(2)}, u32[]{:S(2)}) collective-permute-start(f32[2,512,128]{2,1,0:T(8,128)S(1)} %pad_maximum_fusion.5), channel_id=1, source_target_pairs={{0,64},{1,17},{2,66},{3,19},{4,68},{5,21},{6,70},{7,23},{8,72},{9,... | collective-permute-start | bytes 1572872 | tf_op jit(solution)/shard_map/ppermute | solution.py:58
  57.6 11.3 %collective-permute-start.16 = (f32[256,512]{1,0:T(8,128)S(1)}, f32[256,512]{1,0:T(8,128)S(1)}, u32[]{:S(2)}, u32[]{:S(2)}) collective-permute-start(f32[256,512]{1,0:T(8,128)S(1)} %broadcast_select_fusion.2), channel_id=1, source_target_pairs={{1,97},{8,0},{9,105},{16,24},{17,113},{25,121},{33,65},{40,32},{41... | collective-permute-start | bytes 1572872 | tf_op jit(solution)/shard_map/ppermute | solution.py:58
  61.9 38.3 %collective-permute-start.12 = (f32[2,512,512]{2,1,0:T(8,128)}, f32[2,512,512]{2,1,0:T(8,128)}, u32[]{:S(2)}, u32[]{:S(2)}) collective-permute-start(f32[2,512,512]{2,1,0:T(8,128)} %broadcast_select_fusion), channel_id=1, source_target_pairs={{0,6},{1,3},{2,4},{7,5},{8,14},{9,11},{10,12},{15,13},{16,22},{17,... | collective-permute-start | bytes 6291464 | tf_op jit(solution)/shard_map/ppermute | solution.py:58
  67.4 35.3 %collective-permute-start.10 = (f32[2,2048,128]{2,1,0:T(8,128)S(1)}, f32[2,2048,128]{2,1,0:T(8,128)}, u32[]{:S(2)}, u32[]{:S(2)}) collective-permute-start(f32[2,2048,128]{2,1,0:T(8,128)S(1)} %bitcast.92), channel_id=1, source_target_pairs={{0,24},{1,97},{2,26},{3,99},{4,28},{5,101},{6,30},{7,103},{8,0},{9... | collective-permute-start | bytes 6291464 | tf_op jit(solution)/shard_map/ppermute | solution.py:58
  67.4 35.2 %collective-permute-start.9 = (f32[2,2048,128]{2,1,0:T(8,128)S(1)}, f32[2,2048,128]{2,1,0:T(8,128)}, u32[]{:S(2)}, u32[]{:S(2)}) collective-permute-start(f32[2,2048,128]{2,1,0:T(8,128)S(1)} %bitcast.93), channel_id=1, source_target_pairs={{0,8},{1,33},{2,10},{3,35},{4,12},{5,37},{6,14},{7,39},{8,16},{9,4... | collective-permute-start | bytes 6291464 | tf_op jit(solution)/shard_map/ppermute | solution.py:58
  69.0 0.7 collective-permute-start.17
  70.7 28.3 %collective-permute-start.18 = (f32[256,512]{1,0:T(8,128)}, f32[256,512]{1,0:T(8,128)}, u32[]{:S(2)}, u32[]{:S(2)}) collective-permute-start(f32[256,512]{1,0:T(8,128)} %broadcast_select_fusion.3), channel_id=1, source_target_pairs={{0,6},{1,3},{2,4},{7,5},{8,14},{9,11},{10,12},{15,13},{16,22},{17,... | collective-permute-start | bytes 1572872 | tf_op jit(solution)/shard_map/ppermute | solution.py:58
  75.6 24.7 %copy-start.3 = (f32[2,512,512]{2,1,0:T(8,128)S(1)}, f32[2,512,512]{2,1,0:T(8,128)}, u32[]{:S(2)}) copy-start(f32[2,512,512]{2,1,0:T(8,128)} %shard_map.41) | copy-start | bytes 6291460
  102.9 18.6 %collective-permute-start.19 = (f32[1280,512]{1,0:T(8,128)S(1)}, f32[1280,512]{1,0:T(8,128)S(1)}, u32[]{:S(2)}, u32[]{:S(2)}) collective-permute-start(f32[1280,512]{1,0:T(8,128)S(1)} %pad_maximum_fusion), channel_id=1, source_target_pairs={{0,1},{1,0},{2,3},{3,2},{4,5},{5,4},{6,7},{7,6},{8,9},{9,8},{10,11... | collective-permute-start | bytes 7864328 | tf_op jit(solution)/shard_map/ppermute | solution.py:58
  117.3 20.3 %collective-permute-start.20 = (f32[2048,128]{1,0:T(8,128)S(1)}, f32[2048,128]{1,0:T(8,128)S(1)}, u32[]{:S(2)}, u32[]{:S(2)}) collective-permute-start(f32[2048,128]{1,0:T(8,128)S(1)} %slice_bitcast_fusion.1), channel_id=1, source_target_pairs={{0,8},{1,33},{2,10},{3,35},{4,12},{5,37},{6,14},{7,39},{8,16},{9,4... | collective-permute-start | bytes 3145736 | tf_op jit(solution)/shard_map/ppermute | solution.py:58
  118.7 18.9 %collective-permute-start.21 = (f32[2048,128]{1,0:T(8,128)S(1)}, f32[2048,128]{1,0:T(8,128)S(1)}, u32[]{:S(2)}, u32[]{:S(2)}) collective-permute-start(f32[2048,128]{1,0:T(8,128)S(1)} %slice_bitcast_fusion), channel_id=1, source_target_pairs={{0,24},{1,97},{2,26},{3,99},{4,28},{5,101},{6,30},{7,103},{8,0},{9... | collective-permute-start | bytes 3145736 | tf_op jit(solution)/shard_map/ppermute | solution.py:58
  (2 other events, 5.0 us)
